TPU v7x, 256 devices: a whole 4x4x8 slice. The times are simulated.
256 devices in a mesh: dp: 64 (over x_hi, z, y), tensor: 4 (over x_lo, core).
Axes of the slice: x: 4 (x_hi: 2, x_lo: 2; x = x_hi * 2 + x_lo), y: 4, z: 8, core: 2. Of those that a mesh axis runs over, the one named last changes fastest.
Arguments:
- queries: bfloat16 [32768, 4096], P('dp', 'tensor'), may hold values from -400 to 400
- keys: bfloat16 [32768, 4096], P('dp', 'tensor'), may hold values from -4 to 4
- values: bfloat16 [32768, 4096], P('dp', 'tensor'), may hold values from -6 to 6
- out_grad: bfloat16 [32768, 4096], P('dp', 'tensor'), may hold values from -6 to 6
- layer_input: bfloat16 [32768, 4096], P('dp', 'tensor'), may hold values from -6 to 6
- gate_weight: bfloat16 [4096, 32], P('tensor'), may hold values from -0.09375 to 0.09375
- gate_bias: float32 [32], P('tensor'), may hold values from 3.5 to 10
- doc_lengths: int32 [64], replicated, may hold values from 1 to 1024, 32768 in all
Outputs:
- query_grad: bfloat16 [32768, 4096], P('dp', 'tensor')
- key_grad: bfloat16 [32768, 4096], P('dp', 'tensor')
- value_grad: bfloat16 [32768, 4096], P('dp', 'tensor')
- weight_grad: float32 [4096, 32], P('tensor')
- bias_grad: float32 [32], P('tensor')
Inputs may be any that keep to these rules, and one draw needn't show every extreme that they name: `doc_lengths`: the lengths sum to 32768; the longest document has exactly 1024 tokens.
All inputs are finite; a program needn't handle non-finite values.
Results may differ from a plain program's by a relative error of at most 0.0062.
Values may be sent and summed in bfloat16 or wider, within the bound.
A program may use at most 192 MiB of HBM per device.

v0:
```python
import jax
import jax.numpy as jnp
from jax import lax
from jax.sharding import PartitionSpec as P

SPAN = 2


def prefix(value, axis, combine, identity, reverse):
    count, mine = (lax.axis_size(axis), lax.axis_index(axis))
    everything = lax.all_gather(value, axis)
    start = jnp.broadcast_to(jnp.asarray(identity, value.dtype), value.shape)

    def step(k, before):
        at = count - 1 - k if reverse else k
        reached = at > mine if reverse else at < mine
        new = combine(before, everything[at])
        return jnp.where(reached, new, before)

    return lax.fori_loop(0, count, step, start)


def from_behind(value, axis, steps):
    count = lax.axis_size(axis)
    first, last = (max(0, -steps), min(count, count - steps))
    return lax.ppermute(value, axis, [(source, source + steps) for source in range(first, last)])


def add_terms(earlier, later):
    return earlier + later


def columns_of(array, first_col, size):
    return lax.dynamic_slice_in_dim(array, first_col, size, 1)


def head_terms(
    query_cols,
    key_cols,
    value_cols,
    grad_cols,
    decay_rows,
    decay_keys,
    live_pairs,
    blocks,
    shard_rows,
):
    head_size = query_cols.shape[1]
    scale = head_size ** (-0.5)
    row_count = query_cols.shape[0]
    score = (
        jnp.einsum("qd,kd->qk", query_cols, key_cols, preferred_element_type=jnp.float32) * scale
        + decay_rows[:, None]
        - decay_keys[None, :]
    )
    masked = jnp.where(live_pairs, score, -1e30)
    grouped = masked.reshape(row_count, blocks, shard_rows)
    live_grouped = live_pairs.reshape(row_count, blocks, shard_rows)
    block_top = jnp.max(grouped, axis=2)
    block_unscaled = jnp.where(live_grouped, jnp.exp(grouped - block_top[:, :, None]), 0.0)
    block_sum = jnp.sum(block_unscaled, axis=2)
    block_weight_tile = block_unscaled.astype(jnp.bfloat16)
    value_block_list = value_cols.reshape(blocks, shard_rows, head_size)
    block_output_tile = jnp.einsum(
        "lon,onu->lou", block_weight_tile, value_block_list, preferred_element_type=jnp.float32
    )
    row_peak = jnp.max(block_top, axis=1)
    rescale = jnp.exp(block_top - row_peak[:, None])
    row_total = jnp.sum(block_sum * rescale, axis=1)
    attended = jnp.sum(block_output_tile * rescale[:, :, None], axis=1) / row_total[:, None]
    log_total = row_peak + jnp.log(row_total)
    row_delta = jnp.sum(grad_cols.astype(jnp.float32) * attended, axis=1)
    prob = jnp.where(live_pairs, jnp.exp(masked - log_total[:, None]), 0.0)
    prob_grad = jnp.einsum("qd,kd->qk", grad_cols, value_cols, preferred_element_type=jnp.float32)
    score_grad = prob * (prob_grad - row_delta[:, None])
    score_low = score_grad.astype(jnp.bfloat16)
    prob_low = prob.astype(jnp.bfloat16)
    query_part = jnp.dot(score_low, key_cols, preferred_element_type=jnp.float32) * scale
    key_part = (
        jnp.einsum("qk,qd->kd", score_low, query_cols, preferred_element_type=jnp.float32) * scale
    )
    value_part = jnp.einsum("qk,qd->kd", prob_low, grad_cols, preferred_element_type=jnp.float32)
    return (
        query_part,
        key_part,
        value_part,
        jnp.sum(score_grad, axis=1),
        jnp.sum(score_grad, axis=0),
    )


def shards(queries, keys, values, out_grad, layer_input, gate_weight, gate_bias, doc_lengths):
    shard_rows = queries.shape[0]
    feature_width = queries.shape[1]
    heads_local = gate_bias.shape[0]
    head_size = feature_width // heads_local
    my_index = lax.axis_index("dp")
    doc_ends = jnp.cumsum(doc_lengths)
    own_start = SPAN * shard_rows

    def block_docs(block_index):
        positions = block_index * shard_rows + jnp.arange(shard_rows, dtype=jnp.int32)
        counted = jnp.sum((positions[:, None] >= doc_ends[None, :]).astype(jnp.int32), axis=1)
        return (jnp.where(positions < 0, -1, counted), positions)

    def window_docs(block_index):
        infos = [block_docs(block_index - distance) for distance in range(SPAN, -1, -1)]
        return (
            jnp.concatenate([info[0] for info in infos]),
            jnp.concatenate([info[1] for info in infos]),
        )

    partial_logits = jnp.dot(layer_input, gate_weight, preferred_element_type=jnp.float32)
    gate_logit = (
        lax.psum_scatter(partial_logits, "tensor", scatter_dimension=1, tiled=True) + gate_bias
    )
    log_keep = jax.nn.log_sigmoid(gate_logit)
    head_zeros = jnp.zeros((heads_local,), jnp.float32)
    before = prefix(jnp.sum(log_keep, axis=0), "dp", add_terms, head_zeros, False)
    decay = before + jnp.cumsum(log_keep, axis=0)
    key_value = jnp.stack([keys, values])
    fetched = []
    for distance in range(1, SPAN + 1):
        fetched.append((from_behind(key_value, "dp", distance), from_behind(decay, "dp", distance)))
    ordered = fetched[::-1] + [(key_value, decay)]
    key_window = jnp.concatenate([item[0][0] for item in ordered])
    value_window = jnp.concatenate([item[0][1] for item in ordered])
    decay_window = jnp.concatenate([item[1] for item in ordered])
    doc_window, pos_window = window_docs(my_index)

    def attend(remote_count, query_cols, grad_cols, key_cols, value_cols, decay_cols, doc_w, pos_w):
        first_row = (SPAN - remote_count) * shard_rows
        heads_here = decay_cols.shape[1]
        width_here = query_cols.shape[1]
        doc_q = doc_w[own_start:]
        pos_q = pos_w[own_start:]
        decay_rows = decay_cols[own_start:]
        live_pairs = (doc_q[:, None] == doc_w[None, first_row:]) & (
            pos_w[None, first_row:] <= pos_q[:, None]
        )

        def one_head(head_index):
            first_col = head_index * head_size
            return head_terms(
                columns_of(query_cols, first_col, head_size),
                columns_of(key_cols, first_col, head_size),
                columns_of(value_cols, first_col, head_size),
                columns_of(grad_cols, first_col, head_size),
                columns_of(decay_rows, head_index, 1)[:, 0],
                columns_of(decay_cols, head_index, 1)[:, 0],
                live_pairs,
                remote_count + 1,
                shard_rows,
            )

        query_part, key_part_grad, value_part_grad, row_sum, col_sum = lax.map(
            one_head, jnp.arange(heads_here, dtype=jnp.int32)
        )
        spare = jnp.zeros((first_row, width_here), jnp.float32)
        key_full = jnp.concatenate(
            [spare, key_part_grad.transpose(1, 0, 2).reshape(-1, width_here)]
        )
        value_full = jnp.concatenate(
            [spare, value_part_grad.transpose(1, 0, 2).reshape(-1, width_here)]
        )
        col_full = jnp.concatenate([jnp.zeros((first_row, heads_here), jnp.float32), col_sum.T])
        return (
            query_part.transpose(1, 0, 2).reshape(shard_rows, width_here),
            key_full,
            value_full,
            row_sum.T,
            col_full,
        )

    results = attend(
        SPAN, *(queries, out_grad, key_window, value_window, decay_window, doc_window, pos_window)
    )
    query_grad, key_window_grad, value_window_grad, row_sum, col_window = results
    back_pair = jnp.zeros((2, shard_rows, feature_width), jnp.float32)
    back_col = jnp.zeros((shard_rows, heads_local), jnp.float32)
    for distance in range(1, SPAN + 1):
        lower = (SPAN - distance) * shard_rows
        pair_low = jnp.stack(
            [
                key_window_grad[lower : lower + shard_rows],
                value_window_grad[lower : lower + shard_rows],
            ]
        ).astype(jnp.bfloat16)
        pair_low, column_portion = (pair_low, col_window[lower : lower + shard_rows])
        back_pair = back_pair + from_behind(pair_low, "dp", -distance).astype(jnp.float32)
        back_col = back_col + from_behind(column_portion, "dp", -distance)
    key_grad = key_window_grad[own_start:] + back_pair[0]
    value_grad = value_window_grad[own_start:] + back_pair[1]
    decay_grad = row_sum - (col_window[own_start:] + back_col)
    local_tail = jnp.flip(jnp.cumsum(jnp.flip(decay_grad, 0), axis=0), 0)
    after = prefix(jnp.sum(decay_grad, axis=0), "dp", add_terms, head_zeros, True)
    keep_grad = local_tail + after
    gate_grad = keep_grad * jax.nn.sigmoid(-gate_logit)
    gate_low = gate_grad.astype(jnp.bfloat16)
    all_heads = lax.all_gather(gate_low, "tensor", axis=1, tiled=True)
    weight_term = jnp.einsum(
        "td,th->dh", layer_input, all_heads, preferred_element_type=jnp.float32
    )
    weight_grad, bias_grad = lax.psum((weight_term, jnp.sum(gate_grad, axis=0)), "dp")
    return (
        query_grad.astype(jnp.bfloat16),
        key_grad.astype(jnp.bfloat16),
        value_grad.astype(jnp.bfloat16),
        weight_grad,
        bias_grad,
    )


def solution(mesh):
    return jax.shard_map(
        shards,
        mesh=mesh,
        in_specs=(
            P("dp", "tensor"),
            P("dp", "tensor"),
            P("dp", "tensor"),
            P("dp", "tensor"),
            P("dp", "tensor"),
            P("tensor", None),
            P("tensor"),
            P(),
        ),
        out_specs=(
            P("dp", "tensor"),
            P("dp", "tensor"),
            P("dp", "tensor"),
            P("tensor", None),
            P("tensor"),
        ),
        check_vma=False,
    )
```

profile of v0, /device:TPU:24, one launch (start us, length us, event | category | flops | bytes accessed | tf_op | source)
XLA Modules:
  0.0 1446.3 jit_solution(3617235364206686898)
XLA Ops:
  9.1 4.5 collective-permute-start
  13.6 4.1 collective-permute-start.1
  20.7 92.3 %reduce-scatter.2.cloned.1.call-done = f32[512,8]{0,1:T(8,128)} async-done(((f32[512,32]{0,1:T(8,128)}), f32[512,8]{0,1:T(8,128)}) %reduce-scatter.2.cloned.1.call-update) | async-done | bytes 16400 | tf_op jit(solution)/shard_map/reduce_scatter | solution.py:115
  113.9 159.2 %all-reduce = f32[512]{0:T(512)S(1)} all-reduce(f32[512]{0:T(512)S(1)} %negate_dynamic-update-slice_fusion), channel_id=2, replica_groups=mesh['dp'=64,'tensor'=4] {'dp'}, use_global_device_ids=true, to_apply=%add | all-reduce | flops 512 | bytes 4096
  273.3 2.6 while.50
  279.2 6.0 collective-permute-start.3
  285.3 2.8 collective-permute-done.2
  288.1 2.5 collective-permute-done.3
  294.5 3.1 pad_maximum_fusion
  297.5 236.7 %while.49 = (s32[]{:T(128)}, bf16[8,512,128]{2,1,0:T(8,128)(2,1)S(1)}, f32[8,1536,128]{2,1,0:T(8,128)}, f32[8,1536,128]{2,1,0:T(8,128)}, f32[8,512]{1,0:T(8,128)...) while((s32[]{:T(128)}, ...), condition=%wide.region_19.20_spmd.clone, body=%wide.region_10.19_spmd.clone.sunk | while | flops 1235548672 | bytes 65082244 | solution.py:156
  300.8 3.8 fusion.93
  304.6 3.5 copy.74
  311.9 2.6 fusion.94
  319.7 3.1 fusion.96
  322.8 2.4 fusion.98
  330.3 3.8 fusion.93
  334.1 3.5 copy.74
  341.4 2.6 fusion.94
  349.2 3.2 fusion.96
  352.3 2.4 fusion.98
  359.9 3.8 fusion.93
  363.7 3.5 copy.74
  371.0 2.6 fusion.94
  378.8 3.2 fusion.96
  382.0 2.4 fusion.98
  389.5 3.8 fusion.93
  393.4 3.5 copy.74
  400.6 2.6 fusion.94
  404.2 2.2 fusion.99
  408.5 3.1 fusion.96
  411.6 2.4 fusion.98
  419.2 3.8 fusion.93
  423.0 3.5 copy.74
  430.3 2.6 fusion.94
  438.1 3.1 fusion.96
  441.2 2.4 fusion.98
  448.7 3.8 fusion.93
  452.6 3.5 copy.74
  459.8 2.6 fusion.94
  467.7 3.1 fusion.96
  470.8 2.4 fusion.98
  478.3 3.8 fusion.93
  482.1 3.5 copy.74
  489.4 2.6 fusion.94
  497.2 3.1 fusion.96
  500.4 2.4 fusion.98
  507.9 3.8 fusion.93
  511.7 3.5 copy.74
  519.0 2.6 fusion.94
  526.8 3.1 fusion.96
  529.9 2.5 fusion.98
  534.3 6.5 collective-permute-start.6
  540.8 4.0 collective-permute-start.7
  544.9 3.3 bitcast_convert_fusion.1
  550.3 3.3 bitcast_convert_fusion
  556.6 3.1 pad_maximum_fusion.3
  566.0 2.9 pad_maximum_fusion.4
  572.3 228.4 %all-reduce.1 = f32[512]{0:T(512)S(1)} all-reduce(f32[512]{0:T(512)S(1)} %dynamic-update-slice.1), channel_id=3, replica_groups=mesh['dp'=64,'tensor'=4] {'dp'}, use_global_device_ids=true, to_apply=%add.1 | all-reduce | flops 512 | bytes 4096
  800.8 3.0 while.51
  806.0 5.2 all_gather.16
  812.2 184.9 %psum.15 = f32[8]{0:T(128)} all-reduce(f32[8]{0:T(128)S(1)} %get-tuple-element.438), channel_id=1, replica_groups=mesh['dp'=64,'tensor'=4] {'dp'}, use_global_device_ids=true, to_apply=%region_27.28 | all-reduce | flops 8 | bytes 64 | tf_op jit(solution)/shard_map/psum | solution.py:204
  997.1 2.5 convert_add_fusion
  999.6 4.2 fusion.41
  1003.8 434.1 %all-reduce.4.cloned.1.call-done = f32[1024,32]{0,1:T(8,128)} async-done(((f32[1024,32]{0,1:T(8,128)}), f32[1024,32]{0,1:T(8,128)}) %all-reduce.4.cloned.1.call-update) | async-done | bytes 131088 | tf_op jit(solution)/shard_map/psum | solution.py:204
  (398 shorter events, 122.5 us)
Async XLA Ops:
  7.2 10.5 copy-start
  7.2 12.2 copy-start.12
  7.2 10.5 copy-start.8
  7.2 11.7 copy-start.11
  7.2 105.7 %copy-start.10 = (f32[8]{0:T(128)S(1)}, f32[8]{0:T(128)}, u32[]{:S(2)}) copy-start(f32[8]{0:T(128)} %param.20) | copy-start | bytes 100
  7.2 105.7 %reduce-scatter.2.cloned.1.call-start = ((), (), s32[]{:S(2)}) async-start(), calls=%async_computation.1 | async-start | bytes 81920 | tf_op jit(solution)/shard_map/reduce_scatter | solution.py:115
  9.1 281.5 %collective-permute-start = (bf16[2,512,1024]{2,1,0:T(8,128)(2,1)S(1)}, bf16[2,512,1024]{2,1,0:T(8,128)(2,1)}, u32[]{:S(2)}, u32[]{:S(2)}) collective-permute-start(bf16[2,512,1024]{2,1,0:T(8,128)(2,1)S(1)} %pad_maximum_fusion.2), channel_id=1, source_target_pairs={{0,8},{4,12},{8,16},{12,20},{16,24},{20,28},{24,32},{28,36},{32,40... | collective-permute-start | bytes 6291464 | tf_op jit(solution)/shard_map/ppermute | solution.py:26
  13.6 278.7 %collective-permute-start.1 = (bf16[2,512,1024]{2,1,0:T(8,128)(2,1)S(1)}, bf16[2,512,1024]{2,1,0:T(8,128)(2,1)}, u32[]{:S(2)}, u32[]{:S(2)}) collective-permute-start(bf16[2,512,1024]{2,1,0:T(8,128)(2,1)S(1)} %pad_maximum_fusion.2), channel_id=1, source_target_pairs={{0,4},{4,8},{8,12},{12,16},{16,20},{20,24},{24,28},{28,32},{32,36}... | collective-permute-start | bytes 6291464 | tf_op jit(solution)/shard_map/ppermute | solution.py:26
  18.8 1419.1 %all-reduce.4.cloned.1.call-start = ((), (), s32[]{:S(2)}) async-start(), calls=%async_computation.2 | async-start | bytes 262144 | tf_op jit(solution)/shard_map/psum | solution.py:204
  277.3 10.8 collective-permute-start.2
  279.2 11.4 collective-permute-start.3
  292.3 1.9 copy-start.3
  292.3 2.2 copy-start.4
  294.5 3.1 copy-start.5
  310.3 5.2 copy-start.2
  315.5 3.2 copy-start.1
  339.8 5.2 copy-start.2
  345.0 3.1 copy-start.1
  369.4 5.2 copy-start.2
  374.6 3.2 copy-start.1
  399.0 5.2 copy-start.2
  404.2 3.2 copy-start.1
  428.7 5.2 copy-start.2
  433.9 3.2 copy-start.1
  458.2 5.2 copy-start.2
  463.4 3.2 copy-start.1
  487.8 5.2 copy-start.2
  493.0 3.2 copy-start.1
  517.4 5.2 copy-start.2
  522.6 3.2 copy-start.1
  534.3 10.6 copy-start.6
  534.3 37.7 %collective-permute-start.6 = (f32[512,8]{0,1:T(8,128)S(1)}, f32[512,8]{0,1:T(8,128)S(1)}, u32[]{:S(2)}, u32[]{:S(2)}) collective-permute-start(f32[512,8]{0,1:T(8,128)S(1)} %get-tuple-element.456), channel_id=1, source_target_pairs={{4,0},{8,4},{12,8},{16,12},{20,16},{24,20},{28,24},{32,28},{36,32}... | collective-permute-start | bytes 49160 | tf_op jit(solution)/shard_map/ppermute | solution.py:26
  540.8 31.1 %collective-permute-start.7 = (f32[512,8]{0,1:T(8,128)S(1)}, f32[512,8]{0,1:T(8,128)S(1)}, u32[]{:S(2)}, u32[]{:S(2)}) collective-permute-start(f32[512,8]{0,1:T(8,128)S(1)} %get-tuple-element.455), channel_id=1, source_target_pairs={{8,0},{12,4},{16,8},{20,12},{24,16},{28,20},{32,24},{36,28},{40,32... | collective-permute-start | bytes 49160 | tf_op jit(solution)/shard_map/ppermute | solution.py:26
  559.7 437.4 %collective-permute-start.4 = (bf16[2,512,1024]{2,1,0:T(8,128)(2,1)}, bf16[2,512,1024]{2,1,0:T(8,128)(2,1)}, u32[]{:S(2)}, u32[]{:S(2)}) collective-permute-start(bf16[2,512,1024]{2,1,0:T(8,128)(2,1)} %pad_maximum_fusion.3), channel_id=1, source_target_pairs={{4,0},{8,4},{12,8},{16,12},{20,16},{24,20},{28,24},{32,28},{36,32}... | collective-permute-start | bytes 6291464 | tf_op jit(solution)/shard_map/ppermute | solution.py:26
  566.0 4.8 copy-start.7
  566.0 239.8 %copy-start.9 = (f32[512,8]{0,1:T(8,128)S(1)}, f32[512,8]{0,1:T(8,128)}, u32[]{:S(2)}) copy-start(f32[512,8]{0,1:T(8,128)} %reduce-scatter.2.cloned.1.call-done) | copy-start | bytes 49156
  568.9 428.3 %collective-permute-start.5 = (bf16[2,512,1024]{2,1,0:T(8,128)(2,1)}, bf16[2,512,1024]{2,1,0:T(8,128)(2,1)S(1)}, u32[]{:S(2)}, u32[]{:S(2)}) collective-permute-start(bf16[2,512,1024]{2,1,0:T(8,128)(2,1)} %pad_maximum_fusion.4), channel_id=1, source_target_pairs={{8,0},{12,4},{16,8},{20,12},{24,16},{28,20},{32,24},{36,28},{40,32... | collective-permute-start | bytes 6291464 | tf_op jit(solution)/shard_map/ppermute | solution.py:26
Sparse Core Ops, SparseCore 0:
  18.9 93.9 reduce-scatter.1
  812.3 625.5 all-reduce.3
where the time goes:
time: 1450 us
  blocking collectives  578 us (40%)
  waiting for transfers between devices  532 us (37%)
  matrix products  114 us (8%)
  local copies, waits for them, and re-layouts  76.9 us (5%)
  other arithmetic  74.9 us (5%)
  starting transfers between devices  31 us (2%)
  loops' own time  25.3 us (2%)
  between operations  15.2 us (1%)
    psum x1, waiting for transfers between devices, shards(): lax.psum((weight_term, jnp.sum(gate_grad, axis=0)), 'dp')  434 us
    unnamed x2, blocking collectives  388 us
    psum x1, blocking collectives, shards(): lax.psum((weight_term, jnp.sum(gate_grad, axis=0)), 'dp')  185 us
    reduce_scatter x1, waiting for transfers between devices, shards(): lax.psum_scatter(partial_logits, 'tensor', scatter_dimension=1, tiled=True)  92.3 us
    ppermute x8, starting transfers between devices, from_behind(): lax.ppermute(value, axis, [(source, source + steps) for source in range(f...  30.9 us
    dot_general x8, matrix products, head_terms(): jnp.einsum('qd,kd->qk', query_cols, key_cols, preferred_element_type=jnp....  30.6 us
  transfers between devices with their start and end apart: 10, of which 4 were waited for; matrix products, arithmetic and copies ran while one was open for 3% of the time, Pallas kernels for 0%

commit v1 on v0

v1 whole, which is shorter than its diff:
```python
import functools
import math

import jax
import jax.numpy as jnp
from jax import lax
from jax.experimental import pallas as pl
from jax.experimental.pallas import tpu as pltpu
from jax.sharding import PartitionSpec as P

RING = 4
HALO = 1024
HEAD = 128
TILE = 256
BAND = HALO + TILE
LOG2E = math.log2(math.e)
DEAD = -1e30
MESH = pl.DeviceIdType.MESH
F32 = jnp.float32
BF16 = jnp.bfloat16


def place():
    dp, tensor = lax.axis_index("dp"), lax.axis_index("tensor")
    y = lax.rem(dp, RING)
    return dp, tensor, y, dp - y


def ring_peer(dp, y, step):
    return dp - y + lax.rem(y + step, RING)


def greet(devices):
    barrier = pltpu.get_barrier_semaphore()
    for device in devices:
        pl.semaphore_signal(barrier, inc=1, device_id=device, device_id_type=MESH)
    pl.semaphore_wait(barrier, len(devices))


def send(src, dst, sems, at, device):
    copy = pltpu.make_async_remote_copy(
        src_ref=src,
        dst_ref=dst,
        send_sem=sems[0].at[at],
        recv_sem=sems[1].at[at],
        device_id=device,
        device_id_type=MESH,
    )
    copy.start()
    return copy


def gather_kernel(
    rows, n_dp, n_tensor, q, k, v, g, part, bias,
    qh, kh, vh, gh, logits_out, parts, logits,
    big_send, big_recv, local, halo_send, halo_recv, small_send, small_recv,
):
    dp, tensor, y, ring = place()
    width = 2 * HEAD
    after, before = lax.rem(dp + RING, n_dp), lax.rem(dp + n_dp - RING, n_dp)
    peers = [(ring_peer(dp, y, s), tensor) for s in range(1, RING)]
    mates = [(dp, lax.rem(tensor + s, n_tensor)) for s in range(1, n_tensor)]
    greet(peers + mates + [(after, tensor), (before, tensor)])

    small = (small_send, small_recv)
    outs = [
        send(part.at[pl.ds(pl.multiple_of(mate[1] * 8, 8), 8)], parts.at[s], small, s, mate)
        for s, mate in enumerate(mates)
    ]
    copies, own = {}, []
    for a, (src, dst, first) in enumerate(((k, kh, HALO), (v, vh, HALO), (q, qh, 0), (g, gh, 0))):
        at = pl.ds(pl.multiple_of(first + y * rows, rows), rows)
        for s in (2, 1, 3):
            peer = peers[s - 1]
            there = lax.rem(y + s, RING)
            cols = pl.ds(pl.multiple_of(there * width, width), width)
            copies[a, s] = send(src.at[:, cols], dst.at[at], (big_send, big_recv), a * 3 + s - 1, peer)
        mine = pltpu.make_async_copy(
            src.at[:, pl.ds(pl.multiple_of(y * width, width), width)], dst.at[at], local.at[a]
        )
        mine.start()
        own.append(mine)

    for copy in outs:
        copy.wait()
    total = part[pl.ds(pl.multiple_of(tensor * 8, 8), 8), :] + bias[:, :1]
    for s in range(n_tensor - 1):
        total = total + parts[s]
    logits[2 + y] = total
    outs = [
        send(logits.at[2 + y], logits.at[2 + y], small, 4 + s, peer) for s, peer in enumerate(peers)
    ]
    for copy in outs:
        copy.wait()
    ahead = send(logits.at[4:6], logits.at[0:2], small, 8, (after, tensor))

    for copy in own[:2]:
        copy.wait()
    for a in range(2):
        for s in range(1, RING):
            copies[a, s].wait()
    tail = pl.ds(RING * rows, HALO)
    halo = [
        send(ref.at[tail], ref.at[pl.ds(0, HALO)], (halo_send, halo_recv), a, (after, tensor))
        for a, ref in enumerate((kh, vh))
    ]
    for copy in own[2:]:
        copy.wait()
    for a in range(2, 4):
        for s in range(1, RING):
            copies[a, s].wait()
    ahead.wait()
    for copy in halo:
        copy.wait()
    logits_out[...] = logits[...]


def gather(n_dp, n_tensor, q, k, v, g, part, bias):
    rows = q.shape[0]
    home = RING * rows
    wide = jax.ShapeDtypeStruct((home, 2 * HEAD), BF16)
    long = jax.ShapeDtypeStruct((home + HALO, 2 * HEAD), BF16)
    dma = pltpu.SemaphoreType.DMA
    hbm, vmem = pl.BlockSpec(memory_space=pl.ANY), pl.BlockSpec(memory_space=pltpu.VMEM)
    return pl.pallas_call(
        functools.partial(gather_kernel, rows, n_dp, n_tensor),
        out_shape=(wide, long, long, wide, jax.ShapeDtypeStruct((6, 8, rows), F32)),
        in_specs=[hbm] * 4 + [vmem] * 2,
        out_specs=(hbm, hbm, hbm, hbm, vmem),
        scratch_shapes=[
            pltpu.VMEM((max(1, n_tensor - 1), 8, rows), F32),
            pltpu.VMEM((6, 8, rows), F32),
            dma((12,)), dma((12,)), dma((4,)), dma((2,)), dma((2,)), dma((9,)), dma((9,)),
        ],
        compiler_params=pltpu.CompilerParams(collective_id=0, has_side_effects=True),
        name="gather",
    )(q, k, v, g, part, bias)


def attend_kernel(
    q, k, v, g, decay, starts,
    dq, dk_own, dv_own, dk_halo, dv_halo, row_out, col_out,
    k_t, decay_col, score, grad, dk, dv, col,
):
    scale = HEAD ** (-0.5)
    window = k.shape[0]
    home = q.shape[0]
    chunks = BAND // TILE
    nt = (((1,), (1,)), ((), ()))
    for c in range(window // 512):
        at = slice(c * 512, (c + 1) * 512)
        k_t[:, at] = k[at, :].T
        decay_col[at, :] = decay[0, :, at].T
    dk[...] = jnp.zeros_like(dk)
    dv[...] = jnp.zeros_like(dv)
    col[...] = jnp.zeros_like(col)
    key_at = lax.broadcasted_iota(jnp.int32, (TILE, TILE), 0)
    query_at = lax.broadcasted_iota(jnp.int32, (TILE, TILE), 1)

    def fold(x, combine):
        out = x[:8]
        for r in range(8, x.shape[0], 8):
            out = combine(out, x[r : r + 8])
        return out

    def tile(t, carry):
        base = pl.multiple_of(t * TILE, TILE)
        mine = pl.ds(base, TILE)
        q_t, g_t = q[mine, :], g[mine, :]
        first = starts[0:1, mine] - base
        top = jnp.full((8, TILE), DEAD, F32)
        for c in range(chunks):
            at = pl.ds(base + c * TILE, TILE)
            s = lax.dot_general(k[at, :], q_t, nt, preferred_element_type=F32)
            s = s * (scale * LOG2E) - decay_col[at, 0:1]
            live = key_at >= first - c * TILE
            if c == chunks - 1:
                live = live & (key_at <= query_at)
            s = jnp.where(live, s, DEAD)
            score[c] = s
            top = jnp.maximum(top, fold(s, jnp.maximum))
        top = jnp.max(top, axis=0, keepdims=True)
        total = jnp.zeros((8, TILE), F32)
        delta = jnp.zeros((8, TILE), F32)
        for c in range(chunks):
            at = pl.ds(base + c * TILE, TILE)
            w = jnp.exp2(score[c] - top)
            d = lax.dot_general(v[at, :], g_t, nt, preferred_element_type=F32)
            score[c] = w
            grad[c] = d
            total = total + fold(w, jnp.add)
            delta = delta + fold(w * d, jnp.add)
        inverse = 1.0 / jnp.sum(total, axis=0, keepdims=True)
        delta = jnp.sum(delta, axis=0, keepdims=True) * inverse
        dq_t = jnp.zeros((HEAD, TILE), F32)
        row = jnp.zeros((8, TILE), F32)
        for c in range(chunks):
            at = pl.ds(base + c * TILE, TILE)
            p = score[c] * inverse
            ds = p * (grad[c] - delta)
            low = ds.astype(BF16)
            row = row + fold(ds, jnp.add)
            col[at, :] += ds[:, :HEAD] + ds[:, HEAD:]
            dv[at, :] += jnp.dot(p.astype(BF16), g_t, preferred_element_type=F32)
            dk[at, :] += jnp.dot(low, q_t, preferred_element_type=F32)
            dq_t = dq_t + jnp.dot(k_t[:, at], low, preferred_element_type=F32)
        dq[mine, :] = (dq_t * scale).T.astype(BF16)
        row_out[0, :, mine] = jnp.broadcast_to(jnp.sum(row, axis=0, keepdims=True), (8, TILE))
        return carry

    lax.fori_loop(0, home // TILE, tile, 0)
    dk_halo[...] = (dk[:HALO, :] * scale).astype(BF16)
    dv_halo[...] = dv[:HALO, :].astype(BF16)
    dk_own[...] = dk[HALO:, :] * scale
    dv_own[...] = dv[HALO:, :]
    ones = jnp.ones((8, HEAD), F32)
    col_out[0] = lax.dot_general(
        ones, col[...], nt, precision=lax.Precision.HIGHEST, preferred_element_type=F32
    )


def attend(qh, kh, vh, gh, decay, starts):
    home, window = qh.shape[0], kh.shape[0]
    chunks = BAND // TILE

    def cols(rows):
        return pl.BlockSpec((rows, HEAD), lambda h: (0, h))

    def flat(size):
        return pl.BlockSpec((1, 8, size), lambda h: (h, 0, 0))

    def shape(rows, dtype):
        return jax.ShapeDtypeStruct((rows, 2 * HEAD), dtype)

    return pl.pallas_call(
        attend_kernel,
        grid=(2,),
        out_shape=(
            shape(home, BF16),
            shape(home, F32),
            shape(home, F32),
            shape(HALO, BF16),
            shape(HALO, BF16),
            jax.ShapeDtypeStruct((2, 8, home), F32),
            jax.ShapeDtypeStruct((2, 8, window), F32),
        ),
        in_specs=[
            cols(home), cols(window), cols(window), cols(home), flat(window),
            pl.BlockSpec((8, home), lambda h: (0, 0)),
        ],
        out_specs=(cols(home), cols(home), cols(home), cols(HALO), cols(HALO), flat(home), flat(window)),
        scratch_shapes=[
            pltpu.VMEM((HEAD, window), BF16),
            pltpu.VMEM((window, 8), F32),
            pltpu.VMEM((chunks, TILE, TILE), F32),
            pltpu.VMEM((chunks, TILE, TILE), F32),
            pltpu.VMEM((window, HEAD), F32),
            pltpu.VMEM((window, HEAD), F32),
            pltpu.VMEM((window, HEAD), F32),
        ],
        compiler_params=pltpu.CompilerParams(vmem_limit_bytes=48 * 2**20),
        name="attend",
    )(qh, kh, vh, gh, decay, starts)


def scatter_kernel(
    rows, n_dp, dq, dk_own, dv_own, dk_halo, dv_halo, cols,
    dq_out, dk_out, dv_out, cols_out,
    halo, low, cols_in, big_send, big_recv, local, halo_send, halo_recv,
):
    dp, tensor, y, ring = place()
    width = 2 * HEAD
    home = RING * rows
    after, before = lax.rem(dp + RING, n_dp), lax.rem(dp + n_dp - RING, n_dp)
    peers = [(ring_peer(dp, y, s), tensor) for s in range(1, RING)]
    greet(peers + [(after, tensor), (before, tensor)])
    sems = (halo_send, halo_recv)
    back = [
        send(cols, cols_in, sems, 2, (before, tensor)),
        send(dk_halo, halo.at[0], sems, 0, (before, tensor)),
        send(dv_halo, halo.at[1], sems, 1, (before, tensor)),
    ]
    mine = pl.ds(pl.multiple_of(y * rows, rows), rows)
    here = pl.ds(pl.multiple_of(y * width, width), width)
    waits = []

    def spread(src, dst, a):
        for s in (2, 1, 3):
            there = lax.rem(y + s, RING)
            at = pl.ds(pl.multiple_of(there * rows, rows), rows)
            waits.append(send(src.at[at], dst.at[:, here], (big_send, big_recv), a * 3 + s - 1, peers[s - 1]))
        copy = pltpu.make_async_copy(src.at[mine], dst.at[:, here], local.at[a])
        copy.start()
        waits.append(copy)

    spread(dq, dq_out, 0)
    split = home - HALO
    for a, own in enumerate((dk_own, dv_own)):
        low[a, :split, :] = own[:split, :].astype(BF16)
    for a, (own, out) in enumerate(((dk_own, dk_out), (dv_own, dv_out))):
        back[a + 1].wait()
        low[a, split:, :] = (own[split:, :] + halo[a].astype(F32)).astype(BF16)
        spread(low.at[a], out, a + 1)
    back[0].wait()
    cols_out[...] = cols_in[...]
    for copy in waits:
        copy.wait()


def scatter(n_dp, dq, dk_own, dv_own, dk_halo, dv_halo, cols):
    home = dq.shape[0]
    rows = home // RING
    out = jax.ShapeDtypeStruct((rows, 8 * HEAD), BF16)
    dma = pltpu.SemaphoreType.DMA
    hbm, vmem = pl.BlockSpec(memory_space=pl.ANY), pl.BlockSpec(memory_space=pltpu.VMEM)
    return pl.pallas_call(
        functools.partial(scatter_kernel, rows, n_dp),
        out_shape=(out, out, out, jax.ShapeDtypeStruct(cols.shape, F32)),
        in_specs=[hbm, vmem, vmem, hbm, hbm, vmem],
        out_specs=(hbm, hbm, hbm, vmem),
        scratch_shapes=[
            pltpu.VMEM((2, HALO, 2 * HEAD), BF16),
            pltpu.VMEM((2, home, 2 * HEAD), BF16),
            pltpu.VMEM(cols.shape, F32),
            dma((9,)), dma((9,)), dma((3,)), dma((3,)), dma((3,)),
        ],
        compiler_params=pltpu.CompilerParams(
            collective_id=1, has_side_effects=True, vmem_limit_bytes=48 * 2**20
        ),
        name="scatter",
    )(dq, dk_own, dv_own, dk_halo, dv_halo, cols)


def tail_kernel(
    nz, nx, n_tensor, gate, x, bias,
    weight_out, bias_out,
    gates, wide, term, first, second, third, b_first, b_second, b_third, total, gathered,
    g_send, g_recv, t_send, t_recv, y_send, y_recv, z_send, z_recv, x_send, x_recv, w_send, w_recv, v_send, v_recv,
):
    dp, tensor, y, ring = place()
    part = nz * RING
    xh = dp // part
    z = lax.rem(dp, part) // RING
    peers = [(ring_peer(dp, y, s), tensor) for s in range(1, RING)]
    mates = [(dp, lax.rem(tensor + s, n_tensor)) for s in range(1, n_tensor)]
    line = [(xh * part + lax.rem(z + s, nz) * RING + y, tensor) for s in range(1, nz)]
    cross = [(lax.rem(xh + s, nx) * part + z * RING + y, tensor) for s in range(1, nx)]
    greet(peers + mates + line + cross)

    copies = [
        send(gate.at[lax.rem(y + s + 1, RING)], gates.at[s], (g_send, g_recv), s, peer)
        for s, peer in enumerate(peers)
    ]
    copies_b = [send(bias, b_first.at[s], (g_send, g_recv), 3 + s, peer) for s, peer in enumerate(peers)]
    mine = gate[y]
    for s, copy in enumerate(copies):
        copy.wait()
        mine = mine + gates[s]
    rows = pl.ds(pl.multiple_of(tensor * 8, 8), 8)
    wide[rows, :] = mine
    copies = [
        send(wide.at[rows], wide.at[rows], (t_send, t_recv), s, mate) for s, mate in enumerate(mates)
    ]
    b_sum = bias[...]
    for s, copy in enumerate(copies_b):
        copy.wait()
        b_sum = b_sum + b_first[s]
    total[1] = b_sum
    for copy in copies:
        copy.wait()
    term[...] = jnp.dot(wide[...].astype(BF16), x[...], preferred_element_type=F32)

    block = term.shape[0] // RING
    copies = [
        send(
            term.at[pl.ds(pl.multiple_of(lax.rem(y + s + 1, RING) * block, block), block)],
            first.at[s], (y_send, y_recv), s, peer,
        )
        for s, peer in enumerate(peers)
    ]
    here = pl.ds(pl.multiple_of(y * block, block), block)
    part_sum = term[here, :]
    for s, copy in enumerate(copies):
        copy.wait()
        part_sum = part_sum + first[s]
    term[here, :] = part_sum

    wd = term.shape[1] // nz

    def lanes(at):
        return pl.ds(pl.multiple_of(at * wd, wd), wd)

    copies = [
        send(term.at[here, lanes(lax.rem(z + s + 1, nz))], second.at[s], (z_send, z_recv), s, device)
        for s, device in enumerate(line)
    ]
    copies_b = [
        send(total.at[1], b_second.at[s], (z_send, z_recv), nz - 1 + s, device)
        for s, device in enumerate(line)
    ]
    piece = term[here, lanes(z)]
    for s, copy in enumerate(copies):
        copy.wait()
        piece = piece + second[s]
    for s, copy in enumerate(copies_b):
        copy.wait()
        b_sum = b_sum + b_second[s]
    total[0, :, :wd] = piece
    total[1] = b_sum
    copies = [
        send(total, third.at[s], (x_send, x_recv), s, device) for s, device in enumerate(cross)
    ]
    for s, copy in enumerate(copies):
        copy.wait()
        piece = piece + third[s, 0, :, :wd]
        b_sum = b_sum + third[s, 1]
    bias_out[...] = b_sum

    gathered[here, lanes(z)] = piece
    copies = [
        send(gathered.at[here, lanes(z)], gathered.at[here, lanes(z)], (w_send, w_recv), s, device)
        for s, device in enumerate(line)
    ]
    for copy in copies:
        copy.wait()
    copies = [
        send(gathered.at[here], gathered.at[here], (v_send, v_recv), s, peer)
        for s, peer in enumerate(peers)
    ]
    for copy in copies:
        copy.wait()
    weight_out[...] = gathered[...]


def tail(nz, nx, n_tensor, gate, x, bias):
    heads, width = 8 * n_tensor, x.shape[1]
    rows = gate.shape[2]
    wd = width // nz
    pad = max(wd, 128)
    assert pad == 128 or nz < 8
    block = heads // RING
    dma = pltpu.SemaphoreType.DMA
    vmem = pl.BlockSpec(memory_space=pltpu.VMEM)
    return pl.pallas_call(
        functools.partial(tail_kernel, nz, nx, n_tensor),
        out_shape=(jax.ShapeDtypeStruct((heads, width), F32), jax.ShapeDtypeStruct((8, pad), F32)),
        in_specs=[vmem] * 3,
        out_specs=(vmem, vmem),
        scratch_shapes=[
            pltpu.VMEM((3, 8, rows), F32),
            pltpu.VMEM((heads, rows), F32),
            pltpu.VMEM((heads, width), F32),
            pltpu.VMEM((3, block, width), F32),
            pltpu.VMEM((max(1, nz - 1), block, wd), F32),
            pltpu.VMEM((max(1, nx - 1), 2, 8, pad), F32),
            pltpu.VMEM((3, 8, pad), F32),
            pltpu.VMEM((max(1, nz - 1), 8, pad), F32),
            pltpu.VMEM((1, 8, pad), F32),
            pltpu.VMEM((2, 8, pad), F32),
            pltpu.VMEM((heads, width), F32),
            dma((6,)), dma((6,)), dma((3,)), dma((3,)), dma((3,)), dma((3,)),
            dma((14,)), dma((14,)), dma((1,)), dma((1,)), dma((7,)), dma((7,)), dma((3,)), dma((3,)),
        ],
        compiler_params=pltpu.CompilerParams(collective_id=2, has_side_effects=True),
        name="tail",
    )(gate, x, bias)


def shards(n_dp, n_tensor, q, k, v, g, x, gate_weight, gate_bias, doc_lengths):
    rows = q.shape[0]
    home, window = RING * rows, RING * rows + HALO
    dp, tensor, y, ring = place()
    part = lax.dot_general(gate_weight, x, (((0,), (1,)), ((), ())), preferred_element_type=F32)
    bias = jnp.broadcast_to(gate_bias[:, None], (8, 128))
    qh, kh, vh, gh, logits = gather(n_dp, n_tensor, q, k, v, g, part, bias)

    doc_ends = jnp.cumsum(doc_lengths)
    origin = ring * rows - HALO
    positions = ring * rows + jnp.arange(home, dtype=jnp.int32)
    passed = positions[None, :] >= doc_ends[:, None]
    starts = jnp.max(jnp.where(passed, doc_ends[:, None], 0), axis=0) - origin
    logit = lax.dynamic_slice_in_dim(logits, 2 * y, 2, 1).transpose(1, 0, 2).reshape(2, window)
    decay = jnp.cumsum(jax.nn.log_sigmoid(logit), axis=1) * LOG2E
    decay = jnp.broadcast_to(decay[:, None, :], (2, 8, window))
    dq, dk_own, dv_own, dk_halo, dv_halo, row_sum, col_sum = attend(
        qh, kh, vh, gh, decay, jnp.broadcast_to(starts[None, :], (8, home))
    )

    row_sum, col_sum = row_sum[:, 0], col_sum[:, 0]
    decay_grad = row_sum - col_sum[:, HALO:]
    crossing = jnp.sum(jnp.where(starts[None, :] < HALO, decay_grad, 0.0), axis=1)
    cols = jnp.concatenate([col_sum[:, :HALO], jnp.broadcast_to(crossing[:, None], (2, 128))], axis=1)
    cols = jnp.concatenate([cols, jnp.zeros((6, HALO + 128), F32)])
    query_grad, key_grad, value_grad, cols = scatter(n_dp, dq, dk_own, dv_own, dk_halo, dv_halo, cols)

    decay_grad = decay_grad - jnp.pad(cols[:2, :HALO], ((0, 0), (home - HALO, 0)))
    keep_grad = jnp.flip(jnp.cumsum(jnp.flip(decay_grad, 1), axis=1), 1) + cols[:2, HALO : HALO + 1]
    gate_grad = keep_grad * jax.nn.sigmoid(-logit[:, HALO:])
    low = gate_grad.astype(BF16).astype(F32).reshape(2, RING, rows).transpose(1, 0, 2)
    gate = lax.dynamic_update_slice(jnp.zeros((RING, 8, rows), F32), low, (0, 2 * y, 0))
    nx = 2
    nz = n_dp // (RING * nx)
    pad = max(x.shape[1] // nz, 128)
    sums = jnp.broadcast_to(jnp.sum(gate_grad, axis=1)[:, None], (2, pad))
    sums = lax.dynamic_update_slice(jnp.zeros((8, pad), F32), sums, (2 * y, 0))
    weight, sums = tail(nz, nx, n_tensor, gate, x, sums)
    return query_grad, key_grad, value_grad, weight.T, sums[:, 0]


def solution(mesh):
    return jax.shard_map(
        functools.partial(shards, mesh.shape["dp"], mesh.shape["tensor"]),
        mesh=mesh,
        in_specs=(
            P("dp", "tensor"),
            P("dp", "tensor"),
            P("dp", "tensor"),
            P("dp", "tensor"),
            P("dp", "tensor"),
            P("tensor", None),
            P("tensor"),
            P(),
        ),
        out_specs=(
            P("dp", "tensor"),
            P("dp", "tensor"),
            P("dp", "tensor"),
            P("tensor", None),
            P("tensor"),
        ),
        check_vma=False,
    )
```

time: 1450 us -> 215 us (0.15)
  blocking collectives: 578 us -> 0 us
  waiting for transfers between devices: 532 us -> 0 us
  Pallas kernels: 0 us -> 193 us
  matrix products: 114 us -> 2.28 us
  other arithmetic: 74.9 us -> 3.41 us
  local copies, waits for them, and re-layouts: 76.9 us -> 14.5 us
  starting transfers between devices: 31 us -> 0 us
  loops' own time: 25.3 us -> 0 us
    psum x1 -> x0, waiting for transfers between devices: 434 us -> none  [shards(): lax.psum((weight_term, jnp.sum(gate_grad, axis=0)), 'dp')]
    unnamed x2 -> x0, blocking collectives: 388 us -> none
    pallas_call x0 -> x4, Pallas kernels: none -> 193 us  [the longest x1 83.9 us: gather(): pl.pallas_call(functools.partial(gather_kernel, rows, n_dp, n_tensor), ou...]
    psum x1 -> x0, blocking collectives: 185 us -> none  [shards(): lax.psum((weight_term, jnp.sum(gate_grad, axis=0)), 'dp')]
    dot_general x50 -> x1, matrix products: 114 us -> 2.28 us  [shards(): lax.dot_general(gate_weight, x, (((0,), (1,)), ((), ())), preferred_eleme...]
    reduce_scatter x1 -> x0, waiting for transfers between devices: 92.3 us -> none  [shards(): lax.psum_scatter(partial_logits, 'tensor', scatter_dimension=1, tiled=True)]
    ppermute x8 -> x0, starting transfers between devices: 30.9 us -> none  [from_behind(): lax.ppermute(value, axis, [(source, source + steps) for source in range(f...]
    select_n x8 -> x0, local copies, waits for them, and re-layouts: 28.3 us -> none  [head_terms(): masked = jnp.where(live_pairs, score, -1e+30)]
  transfers between devices with their start and end apart: 10 -> 0, of which waited for: 4 -> 0; matrix products, arithmetic and copies ran while one was open for 3% -> 0% of each run, Pallas kernels for 0% -> 0%
where the time goes in v1:
time: 215 us; the launch traced here: 214 us
  Pallas kernels  193 us (90%)
  local copies, waits for them, and re-layouts  14.5 us (7%)
  other arithmetic  3.41 us (2%)
  matrix products  2.28 us (1%)
    pallas_call x1, Pallas kernels, gather(): pl.pallas_call(functools.partial(gather_kernel, rows, n_dp, n_tensor), ou...  83.9 us
    pallas_call x1, Pallas kernels, scatter(): pl.pallas_call(functools.partial(scatter_kernel, rows, n_dp), out_shape=(...  39.2 us
    pallas_call x1, Pallas kernels, attend(): pl.pallas_call(attend_kernel, grid=(2,), out_shape=(shape(home, BF16), sh...  34.8 us
    pallas_call x1, Pallas kernels, tail(): pl.pallas_call(functools.partial(tail_kernel, nz, nx, n_tensor), out_shap...  34.7 us
    unnamed x21, local copies, waits for them, and re-layouts  8.07 us

profile of v1, /device:TPU:24, one launch (start us, length us, event | category | flops | bytes accessed | tf_op | source)
XLA Modules:
  0.0 213.6 jit_solution(3359721459016163449)
XLA Ops:
  0.6 0.0 copy-start
  0.7 0.8 copy-done
  1.5 2.3 %fusion.4.part = f32[32,512]{1,0:T(8,128)} fusion(bf16[1024,32]{0,1:T(8,128)(2,1)S(1)} %copy-done, bf16[512,1024]{1,0:T(8,128)(2,1)} %x.5), kind=kOutput, calls=%fused_computation.31 | convolution fusion | flops 33554432 | bytes 1179648 | tf_op jit(solution)/shard_map/dot_general | solution.py:473
  3.8 1.3 broadcast_in_dim.36.bias
  5.1 0.0 copy-start.6
  5.1 83.9 %gather.1 = (bf16[2048,256]{1,0:T(8,128)(2,1)}, bf16[3072,256]{1,0:T(8,128)(2,1)}, bf16[3072,256]{1,0:T(8,128)(2,1)}, bf16[2048,256]{1,0:T(8,128)(2,1)}, f32[6,8,512]{2,1,0:T(8,128)}) custom-call(bf16[512,1024]{1,0:T(8,128)(2,1)} %q.1, bf16[512,1024]{1,0:T(8,128)(2,1)} %k.1, bf16[512,1024]{1,0:T(8,128)(2,1)} %v.1, bf16[512,1024]{1,0:T(8,128)(2,1)} %g.1, ...), custom_call_target="tpu_custom_call" | custom-call | tf_op jit(solution)/shard_map/gather/pallas_call | solution.py:125
  89.0 0.9 bitcast_negate_fusion
  89.9 0.6 reduce-window.21
  90.5 0.2 slice_reduce_fusion
  90.7 0.2 reduce-window.24
  90.9 0.1 multiply_bitcast_fusion
  91.0 0.0 copy-done.6
  91.1 0.1 copy.21
  91.2 0.1 reduce-window.30
  91.3 0.1 reduce.1
  91.4 0.2 select_reduce_fusion
  91.6 0.0 copy-start.1
  91.6 1.2 copy-done.1
  92.8 0.0 copy-start.2
  92.8 1.2 copy-done.2
  94.0 34.8 %attend.1 = (bf16[2048,256]{1,0:T(8,128)(2,1)S(1)}, f32[2048,256]{1,0:T(8,128)}, f32[2048,256]{1,0:T(8,128)}, bf16[1024,256]{1,0:T(8,128)(2,1)S(1)}, bf16[1024,2...) custom-call(bf16[2048,256]{1,0:T(8,128)(2,1)S(1)} %copy-done.1, ...), custom_call_target="tpu_custom_call" | custom-call | tf_op jit(solution)/shard_map/attend/pallas_call | solution.py:235
  128.8 0.2 copy.22
  128.9 0.1 copy.23
  129.1 0.1 select_reduce_fusion.1
  129.2 0.1 broadcast_in_dim.42
  129.3 39.2 %scatter.1 = (bf16[512,1024]{1,0:T(8,128)(2,1)S(1)}, bf16[512,1024]{1,0:T(8,128)(2,1)S(1)}, bf16[512,1024]{1,0:T(8,128)(2,1)S(1)}, f32[8,1152]{1,0:T(8,128)S(1)}) custom-call(bf16[2048,256]{1,0:T(8,128)(2,1)S(1)} %get-tuple-element.28.dq, f32[2048,256]{1,0:T(8,128)} %get-tuple-element.29.dk_own, f32[2048,256]{1,0:T(8,128)} %get-tuple-element.30.dv_own, ...), custom_call_target="tpu_custom_call" | custom-call | tf_op jit(solution)/shard_map/scatter/pallas_call | solution.py:316
  168.6 1.4 rev.7
  170.0 0.6 reduce-window.31
  170.6 0.2 slice_reduce_fusion.1
  170.7 0.2 reduce-window.32
  170.9 0.1 add_bitcast_fusion
  171.0 1.4 rev.8
  172.4 0.1 slice_reduce_fusion.3
  172.5 0.2 fusion.3
  172.7 0.1 constant_dynamic-update-slice_fusion.bias
  172.8 0.0 copy-start.5
  172.8 0.6 copy-done.5
  173.4 0.0 copy-start.3
  173.4 0.6 copy-done.3
  174.0 34.7 %tail.1 = (f32[32,1024]{1,0:T(8,128)}, f32[8,128]{1,0:T(8,128)}) custom-call(f32[4,8,512]{2,1,0:T(8,128)} %copy-done.3, bf16[512,1024]{1,0:T(8,128)(2,1)} %x.5, f32[8,128]{1,0:T(8,128)} %copy-done.5), custom_call_target="tpu_custom_call" | custom-call | tf_op jit(solution)/shard_map/tail/pallas_call | solution.py:444
  208.7 1.3 slice_reduce_fusion.2
  210.0 1.0 copy.39
  211.0 0.0 copy-start.4
  211.0 1.0 copy.40
  211.9 1.0 copy.41
  212.9 0.0 copy-done.4
  212.9 0.7 copy.42
  (18 shorter events, 0.2 us)
Async XLA Ops:
  0.6 0.8 copy-start
  5.1 86.0 %copy-start.6 = (s32[64]{0:T(128)S(1)}, s32[64]{0:T(128)}, u32[]{:S(2)}) copy-start(s32[64]{0:T(128)} %param.15) | copy-start | bytes 772
  91.6 1.2 copy-start.1
  92.8 1.2 copy-start.2
  172.8 0.6 copy-start.5
  173.4 0.6 copy-start.3
  211.0 1.9 copy-start.4

commit v2 on v0

v2 whole, which is shorter than its diff:
```python
import functools
import math

import jax
import jax.numpy as jnp
from jax import lax
from jax.experimental import pallas as pl
from jax.experimental.pallas import tpu as pltpu
from jax.sharding import PartitionSpec as P

RING = 4
HALO = 1024
HEAD = 128
TILE = 256
BAND = HALO + TILE
LOG2E = math.log2(math.e)
DEAD = -1e30
MESH = pl.DeviceIdType.MESH
F32 = jnp.float32
BF16 = jnp.bfloat16


def place():
    dp, tensor = lax.axis_index("dp"), lax.axis_index("tensor")
    y = lax.rem(dp, RING)
    return dp, tensor, y, dp - y


def ring_peer(dp, y, step):
    return dp - y + lax.rem(y + step, RING)


def greet(devices):
    barrier = pltpu.get_barrier_semaphore()
    for device in devices:
        pl.semaphore_signal(barrier, inc=1, device_id=device, device_id_type=MESH)
    pl.semaphore_wait(barrier, len(devices))


def send(src, dst, sems, at, device):
    copy = pltpu.make_async_remote_copy(
        src_ref=src,
        dst_ref=dst,
        send_sem=sems[0].at[at],
        recv_sem=sems[1].at[at],
        device_id=device,
        device_id_type=MESH,
    )
    copy.start()
    return copy


def fold(x, combine):
    out = x[:8]
    for r in range(8, x.shape[0], 8):
        out = combine(out, x[r : r + 8])
    return out


def running(chunks, later):
    a = lax.broadcasted_iota(jnp.int32, (128, 128), 0)
    b = lax.broadcasted_iota(jnp.int32, (128, 128), 1)
    ones = jnp.where(a >= b if later else a <= b, 1.0, 0.0).astype(F32)
    sums = jnp.dot(
        jnp.concatenate(chunks), ones, precision=lax.Precision.HIGHEST, preferred_element_type=F32
    )
    return [sums[8 * i : 8 * i + 8] for i in range(len(chunks))]


def tile_step(scale, q, k, v, g, k_t, decay_col, starts, score, grad, dk, dv, col, dq, rows_sum, t):
    chunks = BAND // TILE
    nt = (((1,), (1,)), ((), ()))
    base = pl.multiple_of(t * TILE, TILE)
    mine = pl.ds(base, TILE)
    q_t, g_t = q[mine, :], g[mine, :]
    first = starts[0:1, mine] - base
    key_at = lax.broadcasted_iota(jnp.int32, (TILE, TILE), 0)
    top = jnp.full((8, TILE), DEAD, F32)
    for c in range(chunks):
        at = pl.ds(base + c * TILE, TILE)
        s = lax.dot_general(k[at, :], q_t, nt, preferred_element_type=F32)
        s = s * (scale * LOG2E) - decay_col[at, 0:1]
        live = key_at >= first - c * TILE
        if c == chunks - 1:
            live = live & (key_at <= lax.broadcasted_iota(jnp.int32, (TILE, TILE), 1))
        s = jnp.where(live, s, DEAD)
        score[c] = s
        top = jnp.maximum(top, fold(s, jnp.maximum))
    top = jnp.max(top, axis=0, keepdims=True)
    total = jnp.zeros((8, TILE), F32)
    delta = jnp.zeros((8, TILE), F32)
    for c in range(chunks):
        at = pl.ds(base + c * TILE, TILE)
        w = jnp.exp2(score[c] - top)
        d = lax.dot_general(v[at, :], g_t, nt, preferred_element_type=F32)
        score[c] = w
        grad[c] = d
        total = total + fold(w, jnp.add)
        delta = delta + fold(w * d, jnp.add)
    inverse = 1.0 / jnp.sum(total, axis=0, keepdims=True)
    delta = jnp.sum(delta, axis=0, keepdims=True) * inverse
    dq_t = jnp.zeros((HEAD, TILE), F32)
    row = jnp.zeros((8, TILE), F32)
    for c in range(chunks):
        at = pl.ds(base + c * TILE, TILE)
        p = score[c] * inverse
        ds = p * (grad[c] - delta)
        low = ds.astype(BF16)
        row = row + fold(ds, jnp.add)
        col[at, :] += ds[:, :HEAD] + ds[:, HEAD:]
        dv[at, :] += jnp.dot(p.astype(BF16), g_t, preferred_element_type=F32)
        dk[at, :] += jnp.dot(low, q_t, preferred_element_type=F32)
        dq_t = dq_t + jnp.dot(k_t[:, at], low, preferred_element_type=F32)
    dq[mine, :] = (dq_t * scale).T.astype(BF16)
    rows_sum[:, mine] = jnp.broadcast_to(jnp.sum(row, axis=0, keepdims=True), (8, TILE))


def main_kernel(
    rows, n_dp, n_tensor, nz, nx,
    q, k, v, g, x, gate_weight, gate_bias, lengths,
    dq_out, dk_out, dv_out, weight_out, bias_out,
    qh, kh, vh, gh, parts, part, logits, decay, starts,
    k_t, decay_col, score, grad, dk, dv, col, dq, row_sum, col_sum,
    halo_out, halo_in, low, cols_out, cols_in,
    gate, gates, wide, term, first, second, third, b_first, b_second, b_third, total, gathered,
    in_send, in_recv, own_in, relay_send, relay_recv, small_send, small_recv,
    out_send, out_recv, own_out, halo_send, halo_recv,
    g_send, g_recv, t_send, t_recv, y_send, y_recv, z_send, z_recv, x_send, x_recv, w_send, w_recv, v_send, v_recv,
):
    scale = HEAD ** (-0.5)
    home, window = RING * rows, RING * rows + HALO
    dp, tensor, y, ring = place()
    after, before = lax.rem(dp + RING, n_dp), lax.rem(dp + n_dp - RING, n_dp)
    plane = nz * RING
    xh = dp // plane
    z = lax.rem(dp, plane) // RING
    peers = [(ring_peer(dp, y, s), tensor) for s in range(1, RING)]
    mates = [(dp, lax.rem(tensor + s, n_tensor)) for s in range(1, n_tensor)]
    line = [(xh * plane + lax.rem(z + s, nz) * RING + y, tensor) for s in range(1, nz)]
    cross = [(lax.rem(xh + s, nx) * plane + z * RING + y, tensor) for s in range(1, nx)]
    greet(peers + mates + [(after, tensor), (before, tensor)] + line + cross)

    def columns(shard, h):
        return pl.ds(pl.multiple_of(shard * (2 * HEAD) + h * HEAD, HEAD), HEAD)

    def shard_rows(shard, offset=0):
        return pl.ds(pl.multiple_of(offset + shard * rows, rows), rows)

    arrive, own = {}, {}

    def fetch(h):
        for a, (src, dst, ahead) in enumerate(((k, kh, HALO), (v, vh, HALO), (q, qh, 0), (g, gh, 0))):
            at = shard_rows(y, ahead)
            for s in (2, 1, 3):
                arrive[h, a, s] = send(
                    src.at[:, columns(lax.rem(y + s, RING), h)], dst.at[h, at],
                    (in_send, in_recv), h * 12 + a * 3 + s - 1, peers[s - 1],
                )
            own[h, a] = pltpu.make_async_copy(
                src.at[:, columns(y, h)], dst.at[h, at], own_in.at[h * 4 + a]
            )
            own[h, a].start()

    def arrived(h, arrays):
        for a in arrays:
            own[h, a].wait()
            for s in range(1, RING):
                arrive[h, a, s].wait()

    def relay(h):
        tail = pl.ds(home, HALO)
        return [
            send(ref.at[h, tail], ref.at[h, pl.ds(0, HALO)], (relay_send, relay_recv), h * 2 + a, (after, tensor))
            for a, ref in enumerate((kh, vh))
        ]

    fetch(0)

    part[...] = jnp.dot(x[...], gate_weight[...], preferred_element_type=F32).T
    small = (small_send, small_recv)
    outs = [
        send(part.at[pl.ds(pl.multiple_of(mate[1] * 8, 8), 8)], parts.at[s], small, s, mate)
        for s, mate in enumerate(mates)
    ]
    docs = lengths.shape[1]
    at_0 = lax.broadcasted_iota(jnp.int32, (docs, docs), 0)
    at_1 = lax.broadcasted_iota(jnp.int32, (docs, docs), 1)
    ends = jnp.sum(
        jnp.where(at_1 <= at_0, jnp.broadcast_to(lengths[...], (docs, docs)).astype(F32), 0.0),
        axis=1, keepdims=True,
    ).astype(jnp.int32)
    origin = ring * rows - HALO
    for c in range(home // 512):
        position = ring * rows + c * 512 + lax.broadcasted_iota(jnp.int32, (docs, 512), 1)
        begun = fold(jnp.where(ends <= position, ends, 0), jnp.maximum)
        starts[:, c * 512 : (c + 1) * 512] = jnp.broadcast_to(
            jnp.max(begun, axis=0, keepdims=True) - origin, (8, 512)
        )
    eye = lax.broadcasted_iota(jnp.int32, (8, 8), 0) == lax.broadcasted_iota(jnp.int32, (8, 8), 1)
    bias = jnp.sum(
        jnp.where(eye, jnp.broadcast_to(gate_bias[...], (8, 8)), 0.0), axis=1, keepdims=True
    )
    for copy in outs:
        copy.wait()
    logit = part[pl.ds(pl.multiple_of(tensor * 8, 8), 8), :] + bias
    for s in range(n_tensor - 1):
        logit = logit + parts[s]
    logits[2 + y] = logit
    spread = [
        send(logits.at[2 + y], logits.at[2 + y], small, 3 + s, peer) for s, peer in enumerate(peers)
    ]
    arrived(0, (0, 1))
    relays = relay(0)
    fetch(1)
    for copy in spread:
        copy.wait()
    ahead = send(logits.at[4:6], logits.at[0:2], small, 6, (after, tensor))
    for h in range(2):
        dk[h] = jnp.zeros((window, HEAD), F32)
        dv[h] = jnp.zeros((window, HEAD), F32)
        col[h] = jnp.zeros((window, HEAD), F32)
    ahead.wait()
    pieces = []
    for s in range(6):
        keep = logits[s]
        keep = -(jnp.maximum(-keep, 0.0) + jnp.log1p(jnp.exp(-jnp.abs(keep))))
        pieces += [keep[:, c * 128 : (c + 1) * 128] * LOG2E for c in range(rows // 128)]
    carry = jnp.zeros((8, 1), F32)
    for i, piece in enumerate(running(pieces, False)):
        decay[:, i * 128 : (i + 1) * 128] = piece + carry
        carry = carry + piece[:, 127:128]
    which = lax.broadcasted_iota(jnp.int32, (8, 512), 0)

    def prepare(h, part_of):
        for c in part_of:
            at = slice(c * 512, (c + 1) * 512)
            k_t[:, at] = kh[h, at, :].T
            mine = jnp.where(which == 2 * y + h, decay[:, at], 0.0)
            decay_col[at, :] = jnp.broadcast_to(jnp.sum(mine, axis=0, keepdims=True), (8, 512)).T

    def tiles(h, low_tile, high_tile):
        def step(t, carry):
            tile_step(
                scale, qh.at[h], kh.at[h], vh.at[h], gh.at[h], k_t, decay_col, starts, score, grad,
                dk.at[h], dv.at[h], col.at[h], dq.at[h], row_sum.at[h], t,
            )
            return carry

        lax.fori_loop(low_tile, high_tile, step, 0)

    leave = []

    def give(src, dst, h, a):
        for s in (2, 1, 3):
            leave.append(send(
                src.at[shard_rows(lax.rem(y + s, RING))], dst.at[:, columns(y, h)],
                (out_send, out_recv), h * 9 + a * 3 + s - 1, peers[s - 1],
            ))
        copy = pltpu.make_async_copy(src.at[shard_rows(y)], dst.at[:, columns(y, h)], own_out.at[h * 3 + a])
        copy.start()
        leave.append(copy)

    back = {}

    def give_halo(h):
        halo_out[h, 0] = (dk[h, :HALO, :] * scale).astype(BF16)
        halo_out[h, 1] = dv[h, :HALO, :].astype(BF16)
        for a in range(2):
            back[h, a] = send(
                halo_out.at[h, a], halo_in.at[h, a], (halo_send, halo_recv), h * 2 + a, (before, tensor)
            )

    def give_rest(h):
        split = home - HALO
        for a, (grads, factor, out) in enumerate(((dk, scale, dk_out), (dv, 1.0, dv_out))):
            low[h, a, :split, :] = (grads[h, HALO:home, :] * factor).astype(BF16)
            back[h, a].wait()
            low[h, a, split:, :] = (
                grads[h, home:, :] * factor + halo_in[h, a].astype(F32)
            ).astype(BF16)
            give(low.at[h, a], out, h, a + 1)

    blocks = window // 512
    halo_blocks = HALO // 512
    half = HALO // TILE
    arrived(0, (2, 3))
    prepare(0, range(halo_blocks, blocks))
    tiles(0, half, home // TILE)
    arrived(1, (0, 1))
    relays_1 = relay(1)
    for copy in relays:
        copy.wait()
    prepare(0, range(halo_blocks))
    tiles(0, 0, half)
    give_halo(0)
    give(dq.at[0], dq_out, 0, 0)
    arrived(1, (2, 3))
    for copy in relays_1:
        copy.wait()
    prepare(1, range(blocks))
    tiles(1, 0, half)
    give_halo(1)
    give_rest(0)
    tiles(1, half, home // TILE)
    give(dq.at[1], dq_out, 1, 0)

    nt = (((1,), (1,)), ((), ()))
    ones = jnp.ones((8, HEAD), F32)
    crossed = starts[...] < HALO
    for h in range(2):
        col_sum[h] = lax.dot_general(
            ones, col[h], nt, precision=lax.Precision.HIGHEST, preferred_element_type=F32
        )
        cols_out[h, :, :HALO] = col_sum[h, :, :HALO]
        here = jnp.where(crossed, row_sum[h] - col_sum[h, :, HALO:], 0.0)
        cols_out[h, :, HALO:] = jnp.broadcast_to(jnp.sum(here, axis=1, keepdims=True), (8, 128))
    cols = send(cols_out, cols_in, small, 7, (before, tensor))
    give_rest(1)
    cols.wait()

    which = lax.broadcasted_iota(jnp.int32, (8, 128), 0)
    pieces = []
    for c in range(home // 128):
        at = slice(c * 128, (c + 1) * 128)
        mine = []
        for h in range(2):
            term_h = row_sum[h, :, at] - col_sum[h, :, HALO + c * 128 : HALO + (c + 1) * 128]
            if c >= (home - HALO) // 128:
                off = c * 128 - (home - HALO)
                term_h = term_h - cols_in[h, :, off : off + 128]
            mine.append(term_h)
        pieces.append(jnp.where(which == 2 * y, mine[0], jnp.where(which == 2 * y + 1, mine[1], 0.0)))
    carry = jnp.where(
        which == 2 * y, cols_in[0, :, HALO:], jnp.where(which == 2 * y + 1, cols_in[1, :, HALO:], 0.0)
    )
    bias_sum = jnp.zeros((8, 1), F32)
    sums = running(pieces, True)
    for c in reversed(range(home // 128)):
        shard, off = divmod(c * 128, rows)
        keep = sums[c] + carry
        carry = carry + sums[c][:, 0:1]
        raw = logits[2 + shard, :, off : off + 128]
        down = jnp.exp(-jnp.abs(raw))
        gate_grad = keep * (jnp.where(raw >= 0, down, 1.0) / (1.0 + down))
        bias_sum = bias_sum + jnp.sum(gate_grad, axis=1, keepdims=True)
        gate[shard, :, off : off + 128] = gate_grad.astype(BF16).astype(F32)
    bias_mine = b_third.at[0]
    bias_mine[...] = jnp.broadcast_to(bias_sum, (8, 128))

    copies = [
        send(gate.at[lax.rem(y + s + 1, RING)], gates.at[s], (g_send, g_recv), s, peer)
        for s, peer in enumerate(peers)
    ]
    copies_b = [
        send(bias_mine, b_first.at[s], (g_send, g_recv), 3 + s, peer) for s, peer in enumerate(peers)
    ]
    mine = gate[y]
    for s, copy in enumerate(copies):
        copy.wait()
        mine = mine + gates[s]
    wide_at = pl.ds(pl.multiple_of(tensor * 8, 8), 8)
    wide[wide_at, :] = mine
    copies = [
        send(wide.at[wide_at], wide.at[wide_at], (t_send, t_recv), s, mate) for s, mate in enumerate(mates)
    ]
    b_sum = bias_mine[...]
    for s, copy in enumerate(copies_b):
        copy.wait()
        b_sum = b_sum + b_first[s]
    total[1] = b_sum
    for copy in copies:
        copy.wait()
    term[...] = jnp.dot(wide[...].astype(BF16), x[...], preferred_element_type=F32)

    block = term.shape[0] // RING
    copies = [
        send(
            term.at[pl.ds(pl.multiple_of(lax.rem(y + s + 1, RING) * block, block), block)],
            first.at[s], (y_send, y_recv), s, peer,
        )
        for s, peer in enumerate(peers)
    ]
    here = pl.ds(pl.multiple_of(y * block, block), block)
    part_sum = term[here, :]
    for s, copy in enumerate(copies):
        copy.wait()
        part_sum = part_sum + first[s]
    term[here, :] = part_sum

    wd = term.shape[1] // nz

    def lanes(at):
        return pl.ds(pl.multiple_of(at * wd, wd), wd)

    copies = [
        send(term.at[here, lanes(lax.rem(z + s + 1, nz))], second.at[s], (z_send, z_recv), s, device)
        for s, device in enumerate(line)
    ]
    copies_b = [
        send(total.at[1], b_second.at[s], (z_send, z_recv), nz - 1 + s, device)
        for s, device in enumerate(line)
    ]
    piece = term[here, lanes(z)]
    for s, copy in enumerate(copies):
        copy.wait()
        piece = piece + second[s]
    for s, copy in enumerate(copies_b):
        copy.wait()
        b_sum = b_sum + b_second[s]
    total[0] = piece
    total[1] = b_sum
    copies = [
        send(total, third.at[s], (x_send, x_recv), s, device) for s, device in enumerate(cross)
    ]
    for s, copy in enumerate(copies):
        copy.wait()
        piece = piece + third[s, 0]
        b_sum = b_sum + third[s, 1]
    bias_out[...] = b_sum

    gathered[here, lanes(z)] = piece
    copies = [
        send(gathered.at[here, lanes(z)], gathered.at[here, lanes(z)], (w_send, w_recv), s, device)
        for s, device in enumerate(line)
    ]
    for copy in copies:
        copy.wait()
    copies = [
        send(gathered.at[here], gathered.at[here], (v_send, v_recv), s, peer)
        for s, peer in enumerate(peers)
    ]
    for copy in copies:
        copy.wait()
    weight_out[...] = gathered[...]
    for copy in leave:
        copy.wait()


def shards(n_dp, n_tensor, q, k, v, g, x, gate_weight, gate_bias, doc_lengths):
    rows, width = q.shape
    home, window = RING * rows, RING * rows + HALO
    heads = 8 * n_tensor
    nx = 2
    nz = n_dp // (RING * nx)
    block = heads // RING
    assert width == 128 * nz and block == 8
    chunks = BAND // TILE
    hbm, vmem = pl.BlockSpec(memory_space=pl.ANY), pl.BlockSpec(memory_space=pltpu.VMEM)

    def dma(*sizes):
        return [pltpu.SemaphoreType.DMA((size,)) for size in sizes]

    out = jax.ShapeDtypeStruct((rows, width), BF16)
    pair = [pltpu.VMEM((2, window, HEAD), F32)]
    dq, dk, dv, weight, bias = pl.pallas_call(
        functools.partial(main_kernel, rows, n_dp, n_tensor, nz, nx),
        out_shape=(
            out, out, out,
            jax.ShapeDtypeStruct((heads, width), F32),
            jax.ShapeDtypeStruct((8, 128), F32),
        ),
        in_specs=[hbm] * 4 + [vmem] * 4,
        out_specs=(hbm, hbm, hbm, vmem, vmem),
        scratch_shapes=[
            pltpu.VMEM((2, home, HEAD), BF16),
            pltpu.VMEM((2, window, HEAD), BF16),
            pltpu.VMEM((2, window, HEAD), BF16),
            pltpu.VMEM((2, home, HEAD), BF16),
            pltpu.VMEM((n_tensor - 1, 8, rows), F32),
            pltpu.VMEM((heads, rows), F32),
            pltpu.VMEM((6, 8, rows), F32),
            pltpu.VMEM((8, window), F32),
            pltpu.VMEM((8, home), jnp.int32),
            pltpu.VMEM((HEAD, window), BF16),
            pltpu.VMEM((window, 8), F32),
            pltpu.VMEM((chunks, TILE, TILE), F32),
            pltpu.VMEM((chunks, TILE, TILE), F32),
            *(pair * 3),
            pltpu.VMEM((2, home, HEAD), BF16),
            pltpu.VMEM((2, 8, home), F32),
            pltpu.VMEM((2, 8, window), F32),
            pltpu.VMEM((2, 2, HALO, HEAD), BF16),
            pltpu.VMEM((2, 2, HALO, HEAD), BF16),
            pltpu.VMEM((2, 2, home, HEAD), BF16),
            pltpu.VMEM((2, 8, HALO + 128), F32),
            pltpu.VMEM((2, 8, HALO + 128), F32),
            pltpu.VMEM((RING, 8, rows), F32),
            pltpu.VMEM((3, 8, rows), F32),
            pltpu.VMEM((heads, rows), F32),
            pltpu.VMEM((heads, width), F32),
            pltpu.VMEM((3, block, width), F32),
            pltpu.VMEM((nz - 1, block, 128), F32),
            pltpu.VMEM((nx - 1, 2, 8, 128), F32),
            pltpu.VMEM((3, 8, 128), F32),
            pltpu.VMEM((nz - 1, 8, 128), F32),
            pltpu.VMEM((1, 8, 128), F32),
            pltpu.VMEM((2, 8, 128), F32),
            pltpu.VMEM((heads, width), F32),
            *dma(24, 24, 8, 4, 4, 8, 8),
            *dma(18, 18, 6, 4, 4),
            *dma(6, 6, 3, 3, 3, 3, 2 * (nz - 1), 2 * (nz - 1), 1, 1, nz - 1, nz - 1, 3, 3),
        ],
        compiler_params=pltpu.CompilerParams(
            collective_id=0, has_side_effects=True, vmem_limit_bytes=56 * 2**20
        ),
        name="main",
    )(q, k, v, g, x, gate_weight, gate_bias.reshape(1, 8), doc_lengths.reshape(1, -1))
    return dq, dk, dv, weight.T, bias[:, 0]


def solution(mesh):
    return jax.shard_map(
        functools.partial(shards, mesh.shape["dp"], mesh.shape["tensor"]),
        mesh=mesh,
        in_specs=(
            P("dp", "tensor"),
            P("dp", "tensor"),
            P("dp", "tensor"),
            P("dp", "tensor"),
            P("dp", "tensor"),
            P("tensor", None),
            P("tensor"),
            P(),
        ),
        out_specs=(
            P("dp", "tensor"),
            P("dp", "tensor"),
            P("dp", "tensor"),
            P("tensor", None),
            P("tensor"),
        ),
        check_vma=False,
    )
```

time: 1450 us -> 134 us (0.09)
  blocking collectives: 578 us -> 0 us
  waiting for transfers between devices: 532 us -> 0 us
  Pallas kernels: 0 us -> 124 us
  matrix products: 114 us -> 0 us
  other arithmetic: 74.9 us -> 0 us
  local copies, waits for them, and re-layouts: 76.9 us -> 8.61 us
  starting transfers between devices: 31 us -> 0 us
  loops' own time: 25.3 us -> 0 us
  between operations: 15.2 us -> 0.65 us
    psum x1 -> x0, waiting for transfers between devices: 434 us -> none  [shards(): lax.psum((weight_term, jnp.sum(gate_grad, axis=0)), 'dp')]
    unnamed x2 -> x0, blocking collectives: 388 us -> none
    psum x1 -> x0, blocking collectives: 185 us -> none  [shards(): lax.psum((weight_term, jnp.sum(gate_grad, axis=0)), 'dp')]
    pallas_call x0 -> x1, Pallas kernels: none -> 124 us  [shards(): pl.pallas_call(functools.partial(main_kernel, rows, n_dp, n_tensor, nz, n...]
    dot_general x50 -> x0, matrix products: 114 us -> none  [the longest x8 30.6 us: head_terms(): jnp.einsum('qd,kd->qk', query_cols, key_cols, preferred_element_type=jnp....]
    reduce_scatter x1 -> x0, waiting for transfers between devices: 92.3 us -> none  [shards(): lax.psum_scatter(partial_logits, 'tensor', scatter_dimension=1, tiled=True)]
    ppermute x8 -> x0, starting transfers between devices: 30.9 us -> none  [from_behind(): lax.ppermute(value, axis, [(source, source + steps) for source in range(f...]
    select_n x8 -> x0, local copies, waits for them, and re-layouts: 28.3 us -> none  [head_terms(): masked = jnp.where(live_pairs, score, -1e+30)]
  transfers between devices with their start and end apart: 10 -> 0, of which waited for: 4 -> 0; matrix products, arithmetic and copies ran while one was open for 3% -> 0% of each run, Pallas kernels for 0% -> 0%
where the time goes in v2:
time: 134 us; the launch traced here: 133 us
  Pallas kernels  124 us (93%)
  local copies, waits for them, and re-layouts  8.61 us (6%)
    pallas_call x1, Pallas kernels, shards(): pl.pallas_call(functools.partial(main_kernel, rows, n_dp, n_tensor, nz, n...  124 us
    unnamed x13, local copies, waits for them, and re-layouts  7.99 us

profile of v2, /device:TPU:24, one launch (start us, length us, event | category | flops | bytes accessed | tf_op | source)
XLA Modules:
  0.0 132.8 jit_solution(6147800904344843501)
XLA Ops:
  0.6 1.7 %copy.14.gate_weight = bf16[1024,32]{1,0:T(8,128)(2,1)} copy(bf16[1024,32]{0,1:T(8,128)(2,1)} %param.13) | data formatting | bytes 131072 | tf_op args[5]
  2.3 123.6 %main.1 = (bf16[512,1024]{1,0:T(8,128)(2,1)}, bf16[512,1024]{1,0:T(8,128)(2,1)}, bf16[512,1024]{1,0:T(8,128)(2,1)}, f32[32,1024]{1,0:T(8,128)}, f32[8,128]{1,0:T(8,128)}) custom-call(bf16[512,1024]{1,0:T(8,128)(2,1)} %q.1, bf16[512,1024]{1,0:T(8,128)(2,1)} %k.1, bf16[512,1024]{1,0:T(8,128)(2,1)} %v.1, bf16[512,1024]{1,0:T(8,128)(2,1)} %g.1, ...), custom_call_target="tpu_custom_call" | custom-call | tf_op jit(solution)/shard_map/main/pallas_call | solution.py:455
  125.9 0.0 copy-start.3
  125.9 0.7 copy-done.3
  126.6 0.6 slice_reduce_fusion
  127.2 0.0 copy-start.1
  127.2 2.4 %copy.19 = bf16[512,1024]{1,0:T(8,128)(2,1)} copy(bf16[512,1024]{1,0:T(8,128)(2,1)} %get-tuple-element.20) | data formatting | bytes 2097152
  129.5 0.0 copy-done.1
  129.5 0.0 copy-start
  129.5 1.0 copy.20
  130.5 0.6 copy-done
  131.1 0.0 copy-start.2
  131.1 1.0 copy.21
  132.1 0.1 copy-done.2
  132.2 0.7 copy.22
Async XLA Ops:
  125.9 0.7 copy-start.3
  127.2 2.4 %copy-start.1 = (bf16[512,1024]{1,0:T(8,128)(2,1)S(1)}, bf16[512,1024]{1,0:T(8,128)(2,1)}, u32[]{:S(2)}) copy-start(bf16[512,1024]{1,0:T(8,128)(2,1)} %get-tuple-element.21) | copy-start | bytes 3145732
  129.5 1.6 %copy-start = (bf16[512,1024]{1,0:T(8,128)(2,1)S(1)}, bf16[512,1024]{1,0:T(8,128)(2,1)}, u32[]{:S(2)}) copy-start(bf16[512,1024]{1,0:T(8,128)(2,1)} %get-tuple-element.22) | copy-start | bytes 3145732
  131.1 1.0 copy-start.2

commit v3 on v2

v3 whole, which is shorter than its diff:
```python
import functools
import math

import jax
import jax.numpy as jnp
from jax import lax
from jax.experimental import pallas as pl
from jax.experimental.pallas import tpu as pltpu
from jax.sharding import PartitionSpec as P

RING = 4
HALO = 1024
HEAD = 128
TILE = 256
BAND = HALO + TILE
LOG2E = math.log2(math.e)
DEAD = -1e30
MESH = pl.DeviceIdType.MESH
F32 = jnp.float32
BF16 = jnp.bfloat16


def place():
    dp, tensor = lax.axis_index("dp"), lax.axis_index("tensor")
    y = lax.rem(dp, RING)
    return dp, tensor, y, dp - y


def ring_peer(dp, y, step):
    return dp - y + lax.rem(y + step, RING)


def greet(devices, meanwhile):
    barrier = pltpu.get_barrier_semaphore()
    for device in devices:
        pl.semaphore_signal(barrier, inc=1, device_id=device, device_id_type=MESH)
    meanwhile()
    pl.semaphore_wait(barrier, len(devices))


def send(src, dst, sems, at, device):
    copy = pltpu.make_async_remote_copy(
        src_ref=src,
        dst_ref=dst,
        send_sem=sems[0].at[at],
        recv_sem=sems[1].at[at],
        device_id=device,
        device_id_type=MESH,
    )
    copy.start()
    return copy


def fold(x, combine):
    out = x[:8]
    for r in range(8, x.shape[0], 8):
        out = combine(out, x[r : r + 8])
    return out


def running(chunks, later):
    a = lax.broadcasted_iota(jnp.int32, (128, 128), 0)
    b = lax.broadcasted_iota(jnp.int32, (128, 128), 1)
    ones = jnp.where(a >= b if later else a <= b, 1.0, 0.0).astype(F32)
    sums = jnp.dot(
        jnp.concatenate(chunks), ones, precision=lax.Precision.HIGHEST, preferred_element_type=F32
    )
    return [sums[8 * i : 8 * i + 8] for i in range(len(chunks))]


def tile_step(scale, q, k, v, g, k_t, decay_col, starts, score, grad, dk, dv, col, dq, rows_sum, t):
    chunks = BAND // TILE
    nt = (((1,), (1,)), ((), ()))
    base = pl.multiple_of(t * TILE, TILE)
    mine = pl.ds(base, TILE)
    q_t, g_t = q[mine, :], g[mine, :]
    first = starts[0:1, mine] - base
    key_at = lax.broadcasted_iota(jnp.int32, (TILE, TILE), 0)
    top = jnp.full((8, TILE), DEAD, F32)
    for c in range(chunks):
        at = pl.ds(base + c * TILE, TILE)
        s = lax.dot_general(k[at, :], q_t, nt, preferred_element_type=F32)
        s = s * (scale * LOG2E) - decay_col[at, 0:1]
        live = key_at >= first - c * TILE
        if c == chunks - 1:
            live = live & (key_at <= lax.broadcasted_iota(jnp.int32, (TILE, TILE), 1))
        s = jnp.where(live, s, DEAD)
        score[c] = s
        top = jnp.maximum(top, fold(s, jnp.maximum))
    top = jnp.max(top, axis=0, keepdims=True)
    total = jnp.zeros((8, TILE), F32)
    delta = jnp.zeros((8, TILE), F32)
    for c in range(chunks):
        at = pl.ds(base + c * TILE, TILE)
        w = jnp.exp2(score[c] - top)
        d = lax.dot_general(v[at, :], g_t, nt, preferred_element_type=F32)
        score[c] = w
        grad[c] = d
        total = total + fold(w, jnp.add)
        delta = delta + fold(w * d, jnp.add)
    total = jnp.sum(total, axis=0, keepdims=True)
    inverse = 1.0 / total
    delta = jnp.sum(delta, axis=0, keepdims=True) * inverse
    rows_sum[:, mine] = jnp.broadcast_to(delta - delta * (total * inverse), (8, TILE))
    dq_t = jnp.zeros((HEAD, TILE), F32)
    for c in range(chunks):
        at = pl.ds(base + c * TILE, TILE)
        p = score[c] * inverse
        ds = p * (grad[c] - delta)
        low = ds.astype(BF16)
        col[at, :] += ds[:, :HEAD] + ds[:, HEAD:]
        dv[at, :] += jnp.dot(p.astype(BF16), g_t, preferred_element_type=F32)
        dk[at, :] += jnp.dot(low, q_t, preferred_element_type=F32)
        dq_t = dq_t + jnp.dot(k_t[:, at], low, preferred_element_type=F32)
    dq[mine, :] = (dq_t * scale).T.astype(BF16)


def main_kernel(
    rows, n_dp, n_tensor, nz, nx,
    q, k, v, g, x_in, gate_weight, gate_bias, lengths,
    dq_out, dk_out, dv_out, weight_out, bias_out,
    qh, kh, vh, gh, parts, part, logits, decay, starts,
    k_t, decay_col, score, grad, dk, dv, col, dq, row_sum, col_sum,
    halo_out, halo_in, low, cols_out, cols_in,
    gate, inbox, wide, term, first, stage, second, x, x_sem,
    in_send, in_recv, own_in, relay_send, relay_recv, small_send, small_recv,
    out_send, out_recv, own_out, halo_send, halo_recv,
    g_send, g_recv, y_send, y_recv, z_send, z_recv, w_send, w_recv, v_send, v_recv,
):
    scale = HEAD ** (-0.5)
    home, window = RING * rows, RING * rows + HALO
    dp, tensor, y, ring = place()
    after, before = lax.rem(dp + RING, n_dp), lax.rem(dp + n_dp - RING, n_dp)
    plane = nz * RING
    xh = dp // plane
    z = lax.rem(dp, plane) // RING
    peers = [(ring_peer(dp, y, s), tensor) for s in range(1, RING)]
    mates = [(dp, lax.rem(tensor + s, n_tensor)) for s in range(1, n_tensor)]
    line = [(xh * plane + lax.rem(z + s, nz) * RING + y, tensor) for s in range(1, nz)]
    planes = [
        (lax.rem(xh + a, nx) * plane + lax.rem(z + b, nz) * RING + y, tensor)
        for a in range(nx)
        for b in range(nz)
    ][1:]
    homes = [
        (ring_peer(dp, y, a), lax.rem(tensor + b, n_tensor)) for a in range(RING) for b in range(n_tensor)
    ][1:]
    x_copy = pltpu.make_async_copy(x_in, x, x_sem)
    x_copy.start()

    def meanwhile():
        x_copy.wait()
        part[...] = lax.dot_general(
            gate_weight[...], x[...], (((1,), (1,)), ((), ())), preferred_element_type=F32
        )

    greet(homes + planes, meanwhile)

    def columns(shard, h):
        return pl.ds(pl.multiple_of(shard * (2 * HEAD) + h * HEAD, HEAD), HEAD)

    def shard_rows(shard, offset=0):
        return pl.ds(pl.multiple_of(offset + shard * rows, rows), rows)

    arrive, own = {}, {}

    def fetch(h, arrays):
        for a in arrays:
            src, dst, ahead = ((k, kh, HALO), (v, vh, HALO), (q, qh, 0), (g, gh, 0))[a]
            at = shard_rows(y, ahead)
            for s in (2, 1, 3):
                arrive[h, a, s] = send(
                    src.at[:, columns(lax.rem(y + s, RING), h)], dst.at[h, at],
                    (in_send, in_recv), h * 12 + a * 3 + s - 1, peers[s - 1],
                )
            own[h, a] = pltpu.make_async_copy(
                src.at[:, columns(y, h)], dst.at[h, at], own_in.at[h * 4 + a]
            )
            own[h, a].start()

    def arrived(h, arrays):
        for a in arrays:
            own[h, a].wait()
            for s in range(1, RING):
                arrive[h, a, s].wait()

    def relay(h):
        tail = pl.ds(home, HALO)
        return [
            send(ref.at[h, tail], ref.at[h, pl.ds(0, HALO)], (relay_send, relay_recv), h * 2 + a, (after, tensor))
            for a, ref in enumerate((kh, vh))
        ]


    small = (small_send, small_recv)
    outs = [
        send(part.at[pl.ds(pl.multiple_of(mate[1] * 8, 8), 8)], parts.at[s], small, s, mate)
        for s, mate in enumerate(mates)
    ]
    fetch(0, (0,))
    eye = lax.broadcasted_iota(jnp.int32, (8, 8), 0) == lax.broadcasted_iota(jnp.int32, (8, 8), 1)
    bias = jnp.sum(
        jnp.where(eye, jnp.broadcast_to(gate_bias[...], (8, 8)), 0.0), axis=1, keepdims=True
    )
    for copy in outs:
        copy.wait()
    logit = part[pl.ds(pl.multiple_of(tensor * 8, 8), 8), :] + bias
    for s in range(n_tensor - 1):
        logit = logit + parts[s]
    logits[2 + y] = logit
    spread = [
        send(logits.at[2 + y], logits.at[2 + y], small, 3 + s, peer) for s, peer in enumerate(peers)
    ]
    fetch(0, (1, 2, 3))
    fetch(1, range(4))
    docs = lengths.shape[1]
    at_0 = lax.broadcasted_iota(jnp.int32, (docs, docs), 0)
    at_1 = lax.broadcasted_iota(jnp.int32, (docs, docs), 1)
    ends = jnp.sum(
        jnp.where(at_1 <= at_0, jnp.broadcast_to(lengths[...], (docs, docs)).astype(F32), 0.0),
        axis=1, keepdims=True,
    ).astype(jnp.int32)
    origin = ring * rows - HALO
    for c in range(home // 512):
        position = ring * rows + c * 512 + lax.broadcasted_iota(jnp.int32, (docs, 512), 1)
        begun = fold(jnp.where(ends <= position, ends, 0), jnp.maximum)
        starts[:, c * 512 : (c + 1) * 512] = jnp.broadcast_to(
            jnp.max(begun, axis=0, keepdims=True) - origin, (8, 512)
        )
    for copy in spread:
        copy.wait()
    ahead = send(logits.at[4:6], logits.at[0:2], small, 6, (after, tensor))
    for h in range(2):
        dk[h] = jnp.zeros((window, HEAD), F32)
        dv[h] = jnp.zeros((window, HEAD), F32)
        col[h] = jnp.zeros((window, HEAD), F32)
    arrived(0, (0, 1))
    relays = relay(0)
    ahead.wait()
    pieces = []
    for s in range(6):
        keep = logits[s]
        keep = -(jnp.maximum(-keep, 0.0) + jnp.log1p(jnp.exp(-jnp.abs(keep))))
        pieces += [keep[:, c * 128 : (c + 1) * 128] * LOG2E for c in range(rows // 128)]
    carry = jnp.zeros((8, 1), F32)
    for i, piece in enumerate(running(pieces, False)):
        decay[:, i * 128 : (i + 1) * 128] = piece + carry
        carry = carry + piece[:, 127:128]
    which = lax.broadcasted_iota(jnp.int32, (8, 512), 0)

    def prepare(h, part_of):
        for c in part_of:
            at = slice(c * 512, (c + 1) * 512)
            k_t[:, at] = kh[h, at, :].T
            mine = jnp.where(which == 2 * y + h, decay[:, at], 0.0)
            decay_col[at, :] = jnp.broadcast_to(jnp.sum(mine, axis=0, keepdims=True), (8, 512)).T

    def tiles(h, low_tile, high_tile):
        def step(t, carry):
            tile_step(
                scale, qh.at[h], kh.at[h], vh.at[h], gh.at[h], k_t, decay_col, starts, score, grad,
                dk.at[h], dv.at[h], col.at[h], dq.at[h], row_sum.at[h], t,
            )
            return carry

        lax.fori_loop(low_tile, high_tile, step, 0)

    leave = []

    def give(src, dst, h, a, shards_of):
        def to(s):
            return pltpu.make_async_remote_copy(
                src_ref=src.at[shard_rows(lax.rem(y + s, RING))],
                dst_ref=dst.at[:, columns(y, h)],
                send_sem=out_send.at[h * 9 + a * 3 + s - 1],
                recv_sem=out_recv.at[h * 9 + a * 3 + s - 1],
                device_id=(ring_peer(dp, y, s), tensor),
                device_id_type=MESH,
            )

        copy = pltpu.make_async_copy(src.at[shard_rows(y)], dst.at[:, columns(y, h)], own_out.at[h * 3 + a])
        for s in (2, 1, 3):
            there = lax.rem(y + s, RING)
            pl.when((there >= shards_of[0]) & (there < shards_of[1]))(to(s).start)
        pl.when((y >= shards_of[0]) & (y < shards_of[1]))(copy.start)
        if shards_of[0] == 0:
            leave.extend([to(1), to(2), to(3), copy])

    back = {}

    def give_halo(h):
        halo_out[h, 0] = (dk[h, :HALO, :] * scale).astype(BF16)
        halo_out[h, 1] = dv[h, :HALO, :].astype(BF16)
        for a in range(2):
            back[h, a] = send(
                halo_out.at[h, a], halo_in.at[h, a], (halo_send, halo_recv), h * 2 + a, (before, tensor)
            )

    grads = ((dk, scale, dk_out), (dv, 1.0, dv_out))
    split = home - HALO
    near, far = (0, split // rows), (split // rows, RING)

    def cast_near(h):
        for a, (of, factor, _) in enumerate(grads):
            low[h, a, :split, :] = (of[h, HALO:home, :] * factor).astype(BF16)

    def give_near(h, arrays=(0, 1)):
        for a in arrays:
            out = grads[a][2]
            give(low.at[h, a], out, h, a + 1, near)

    def give_far(h):
        for a, (of, factor, out) in enumerate(grads):
            back[h, a].wait()
            low[h, a, split:, :] = (
                of[h, home:, :] * factor + halo_in[h, a].astype(F32)
            ).astype(BF16)
            give(low.at[h, a], out, h, a + 1, far)

    def sum_columns(h):
        col_sum[h] = lax.dot_general(
            jnp.ones((8, HEAD), F32), col[h], (((1,), (1,)), ((), ())),
            precision=lax.Precision.HIGHEST, preferred_element_type=F32,
        )

    blocks = window // 512
    halo_blocks = HALO // 512
    half = HALO // TILE
    full = home // TILE
    prepare(0, range(halo_blocks, blocks))
    arrived(0, (2, 3))
    tiles(0, half, full)
    for copy in relays:
        copy.wait()
    prepare(0, range(halo_blocks))
    tiles(0, 0, half // 2)
    arrived(1, (0, 1))
    relays_1 = relay(1)
    tiles(0, half // 2, half)
    give_halo(0)
    cast_near(0)
    give(dq.at[0], dq_out, 0, 0, (0, RING))
    give_near(0)
    sum_columns(0)
    prepare(1, range(halo_blocks, blocks))
    arrived(1, (2, 3))
    tiles(1, half, full)
    for copy in relays_1:
        copy.wait()
    prepare(1, range(halo_blocks))
    give_far(0)
    tiles(1, 0, half)

    sum_columns(1)
    which = lax.broadcasted_iota(jnp.int32, (8, 128), 0)
    crossed = starts[...] < HALO
    over = []
    for h in range(2):
        here = jnp.where(crossed, row_sum[h] - col_sum[h, :, HALO:], 0.0)
        over.append(jnp.broadcast_to(jnp.sum(here, axis=1, keepdims=True), (8, 128)))
    for c in range(HALO // 128):
        at = slice(c * 128, (c + 1) * 128)
        cols_out[:, at] = jnp.where(which == 0, col_sum[0, :, at], col_sum[1, :, at])
    cols_out[:, HALO:] = jnp.where(which == 0, over[0], over[1])
    cols = send(cols_out, cols_in, small, 7, (before, tensor))
    give_halo(1)
    cast_near(1)
    cols.wait()

    pieces, packed = {}, {}
    bias_sum = jnp.zeros((8, 1), F32)
    for h in range(2):
        for c in range(home // 128):
            at = slice(c * 128, (c + 1) * 128)
            piece = row_sum[h, :, at] - col_sum[h, :, HALO + c * 128 : HALO + (c + 1) * 128]
            if c * 128 >= split:
                off = c * 128 - split
                piece = piece - cols_in[h : h + 1, off : off + 128]
            pieces[h, c] = piece
    sums = dict(zip(pieces, running(list(pieces.values()), True)))
    for h in range(2):
        carry = cols_in[h : h + 1, HALO : HALO + 1]
        mine_of = jnp.zeros((8, 1), F32)
        for c in reversed(range(home // 128)):
            shard, off = divmod(c * 128, rows)
            keep = sums[h, c] + carry
            carry = carry + sums[h, c][:, 0:1]
            raw = logits[2 + shard, :, off : off + 128]
            raw = jnp.sum(jnp.where(which == 2 * y + h, raw, 0.0), axis=0, keepdims=True)
            down = jnp.exp(-jnp.abs(raw))
            gate_grad = keep * (jnp.where(raw >= 0, down, 1.0) / (1.0 + down))
            mine_of = mine_of + jnp.sum(gate_grad, axis=1, keepdims=True)
            row = h * (rows // 128) + off // 128
            packed[shard] = jnp.where(which == row, gate_grad, packed.get(shard, 0.0))
        bias_sum = jnp.where(which[:, :1] == 2 * y + h, mine_of, bias_sum)
    for shard in range(RING):
        gate[shard] = packed[shard].astype(BF16).astype(F32)

    slot = tensor * RING + y
    copies = [
        send(gate.at[lax.rem(device[0], RING)], inbox.at[slot], (g_send, g_recv), s, device)
        for s, device in enumerate(homes)
    ]
    give(dq.at[1], dq_out, 1, 0, (0, RING))
    give_near(1, (0,))
    inbox[slot] = gate[y]
    for copy in copies:
        copy.wait()
    for s in range(n_tensor * RING):
        for r in range(8):
            h, c = divmod(r, rows // 128)
            wide[2 * s + h : 2 * s + h + 1, c * 128 : (c + 1) * 128] = inbox[s, r : r + 1, :]
    width = x.shape[1]
    term[:, :width] = jnp.dot(wide[...].astype(BF16), x[...], preferred_element_type=F32)
    for r in range(0, term.shape[0], 8):
        term[r : r + 8, width:] = jnp.broadcast_to(bias_sum, (8, 128))

    copies = [
        send(
            term.at[pl.ds(pl.multiple_of(lax.rem(device[0], RING) * 8, 8), 8)],
            first.at[s], (y_send, y_recv), s, device,
        )
        for s, device in enumerate(peers)
    ]
    give_near(1, (1,))
    here = pl.ds(pl.multiple_of(y * 8, 8), 8)
    part_sum = term[here, :]
    for s, copy in enumerate(copies):
        copy.wait()
        part_sum = part_sum + first[s]
    for c in range(nz):
        stage[c, :, :128] = part_sum[:, c * 128 : (c + 1) * 128]
        stage[c, :, 128:] = part_sum[:, width:]

    copies = [
        send(stage.at[lax.rem(device[0], plane) // RING], second.at[s], (z_send, z_recv), s, device)
        for s, device in enumerate(planes)
    ]
    give_far(1)
    piece = stage[z]
    for s, copy in enumerate(copies):
        copy.wait()
        piece = piece + second[s]
    eye = which == lax.broadcasted_iota(jnp.int32, (8, 128), 1)
    bias_out[...] = jnp.sum(jnp.where(eye, piece[:, 128:], 0.0), axis=0, keepdims=True)[:, :8]

    lanes = pl.ds(pl.multiple_of(z * 128, 128), 128)
    weight_out[here, lanes] = piece[:, :128]
    copies = [
        send(weight_out.at[here, lanes], weight_out.at[here, lanes], (w_send, w_recv), s, device)
        for s, device in enumerate(line)
    ]
    for copy in copies:
        copy.wait()
    copies = [
        send(weight_out.at[here], weight_out.at[here], (v_send, v_recv), s, device)
        for s, device in enumerate(peers)
    ]
    for copy in copies:
        copy.wait()
    for copy in leave:
        copy.wait()


def finish_kernel(*refs):
    count = len(refs) // 3
    ins, outs, held = refs[:count], refs[count : 2 * count], refs[2 * count : 3 * count]
    load, store = refs[3 * count :]
    loads = [pltpu.make_async_copy(ins[i], held[i], load.at[i]) for i in range(count)]
    stores = [pltpu.make_async_copy(held[i], outs[i], store.at[i]) for i in range(count)]
    for copy in loads:
        copy.start()
    for i in range(count):
        loads[i].wait()
        stores[i].start()
    for copy in stores:
        copy.wait()


def finish(*arrays):
    hbm = pl.BlockSpec(memory_space=pl.ANY)
    return pl.pallas_call(
        finish_kernel,
        out_shape=tuple(jax.ShapeDtypeStruct(a.shape, a.dtype) for a in arrays),
        in_specs=[hbm] * len(arrays),
        out_specs=(hbm,) * len(arrays),
        scratch_shapes=[pltpu.VMEM(a.shape, a.dtype) for a in arrays]
        + [pltpu.SemaphoreType.DMA((len(arrays),))] * 2,
        compiler_params=pltpu.CompilerParams(vmem_limit_bytes=56 * 2**20),
        name="finish",
    )(*arrays)


def shards(n_dp, n_tensor, q, k, v, g, x, gate_weight, gate_bias, doc_lengths):
    rows, width = q.shape
    home, window = RING * rows, RING * rows + HALO
    heads = 8 * n_tensor
    nx = 2
    nz = n_dp // (RING * nx)
    assert width == 128 * nz and heads == 8 * RING and rows == 512
    chunks = BAND // TILE
    hbm, vmem = pl.BlockSpec(memory_space=pl.ANY), pl.BlockSpec(memory_space=pltpu.VMEM)

    def dma(*sizes):
        return [pltpu.SemaphoreType.DMA((size,)) for size in sizes]

    out = jax.ShapeDtypeStruct((rows, width), BF16)
    pair = [pltpu.VMEM((2, window, HEAD), F32)]
    dq, dk, dv, weight, bias = pl.pallas_call(
        functools.partial(main_kernel, rows, n_dp, n_tensor, nz, nx),
        out_shape=(
            out, out, out,
            jax.ShapeDtypeStruct((heads, width), F32),
            jax.ShapeDtypeStruct((1, 8), F32),
        ),
        in_specs=[hbm] * 5 + [vmem] * 3,
        out_specs=(hbm, hbm, hbm, vmem, vmem),
        scratch_shapes=[
            pltpu.VMEM((2, home, HEAD), BF16),
            pltpu.VMEM((2, window, HEAD), BF16),
            pltpu.VMEM((2, window, HEAD), BF16),
            pltpu.VMEM((2, home, HEAD), BF16),
            pltpu.VMEM((n_tensor - 1, 8, rows), F32),
            pltpu.VMEM((heads, rows), F32),
            pltpu.VMEM((6, 8, rows), F32),
            pltpu.VMEM((8, window), F32),
            pltpu.VMEM((8, home), jnp.int32),
            pltpu.VMEM((HEAD, window), BF16),
            pltpu.VMEM((window, 8), F32),
            pltpu.VMEM((chunks, TILE, TILE), F32),
            pltpu.VMEM((chunks, TILE, TILE), F32),
            *(pair * 3),
            pltpu.VMEM((2, home, HEAD), BF16),
            pltpu.VMEM((2, 8, home), F32),
            pltpu.VMEM((2, 8, window), F32),
            pltpu.VMEM((2, 2, HALO, HEAD), BF16),
            pltpu.VMEM((2, 2, HALO, HEAD), BF16),
            pltpu.VMEM((2, 2, home, HEAD), BF16),
            pltpu.VMEM((8, HALO + 128), F32),
            pltpu.VMEM((8, HALO + 128), F32),
            pltpu.VMEM((RING, 8, 128), F32),
            pltpu.VMEM((n_tensor * RING, 8, 128), F32),
            pltpu.VMEM((heads, rows), F32),
            pltpu.VMEM((heads, width + 128), F32),
            pltpu.VMEM((3, 8, width + 128), F32),
            pltpu.VMEM((nz, 8, 256), F32),
            pltpu.VMEM((nx * nz - 1, 8, 256), F32),
            pltpu.VMEM((rows, width), BF16),
            pltpu.SemaphoreType.DMA,
            *dma(24, 24, 8, 4, 4, 8, 8),
            *dma(18, 18, 6, 4, 4),
            *dma(*[n_tensor * RING - 1] * 2, 3, 3, *[nx * nz - 1] * 2, nz - 1, nz - 1, 3, 3),
        ],
        compiler_params=pltpu.CompilerParams(
            collective_id=0, has_side_effects=True, vmem_limit_bytes=56 * 2**20
        ),
        name="main",
    )(q, k, v, g, x, gate_weight.T, gate_bias.reshape(1, 8), doc_lengths.reshape(1, -1))
    dq, dk, dv, weight, bias = finish(dq, dk, dv, weight, bias)
    return dq, dk, dv, weight.T, bias.reshape(8)


def solution(mesh):
    return jax.shard_map(
        functools.partial(shards, mesh.shape["dp"], mesh.shape["tensor"]),
        mesh=mesh,
        in_specs=(
            P("dp", "tensor"),
            P("dp", "tensor"),
            P("dp", "tensor"),
            P("dp", "tensor"),
            P("dp", "tensor"),
            P("tensor", None),
            P("tensor"),
            P(),
        ),
        out_specs=(
            P("dp", "tensor"),
            P("dp", "tensor"),
            P("dp", "tensor"),
            P("tensor", None),
            P("tensor"),
        ),
        check_vma=False,
    )
```

time: 134 us -> 117 us (0.87)
  local copies, waits for them, and re-layouts: 8.61 us -> 0 us
  Pallas kernels: 124 us -> 116 us
    pallas_call x1, Pallas kernels: 124 us -> 113 us  [shards(): pl.pallas_call(functools.partial(main_kernel, rows, n_dp, n_tensor, nz, n...]
    unnamed x13 -> x0, local copies, waits for them, and re-layouts: 7.99 us -> none
    pallas_call x0 -> x1, Pallas kernels: none -> 3.01 us  [finish(): pl.pallas_call(finish_kernel, out_shape=tuple((jax.ShapeDtypeStruct(a.sha...]
where the time goes in v3:
time: 117 us; the launch traced here: 116 us
  Pallas kernels  116 us (99%)
    pallas_call x1, Pallas kernels, shards(): pl.pallas_call(functools.partial(main_kernel, rows, n_dp, n_tensor, nz, n...  113 us
    pallas_call x1, Pallas kernels, finish(): pl.pallas_call(finish_kernel, out_shape=tuple((jax.ShapeDtypeStruct(a.sha...  3.01 us

profile of v3, /device:TPU:24, one launch (start us, length us, event | category | flops | bytes accessed | tf_op | source)
XLA Modules:
  0.0 116.3 jit_solution(13183273001465058365)
XLA Ops:
  0.6 112.7 %main.1 = (bf16[512,1024]{1,0:T(8,128)(2,1)}, bf16[512,1024]{1,0:T(8,128)(2,1)}, bf16[512,1024]{1,0:T(8,128)(2,1)}, f32[32,1024]{1,0:T(8,128)}, f32[1,8]{1,0:T(1,128)}) custom-call(bf16[512,1024]{1,0:T(8,128)(2,1)} %q.1, bf16[512,1024]{1,0:T(8,128)(2,1)} %k.1, bf16[512,1024]{1,0:T(8,128)(2,1)} %v.1, bf16[512,1024]{1,0:T(8,128)(2,1)} %g.1, ...), custom_call_target="tpu_custom_call" | custom-call | tf_op jit(solution)/shard_map/main/pallas_call | solution.py:509
  113.3 3.0 %finish.1 = (bf16[512,1024]{1,0:T(8,128)(2,1)}, bf16[512,1024]{1,0:T(8,128)(2,1)}, bf16[512,1024]{1,0:T(8,128)(2,1)}, f32[32,1024]{1,0:T(8,128)}, f32[1,8]{1,0:T(1,128)}) custom-call(bf16[512,1024]{1,0:T(8,128)(2,1)} %get-tuple-element.15.refs_0_, bf16[512,1024]{1,0:T(8,128)(2,1)} %get-tuple-element.16.refs_1_, bf16[512,1024]{1,0:T(8,128)(2,1)} %get-tuple-element.17.refs_2_, ...), custom_call_target="tpu_custom_call" | custom-call | tf_op jit(solution)/shard_map/finish/pallas_call | solution.py:482

commit v4 on v3

--- a/solution.py
+++ b/solution.py
@@ -68,7 +68,7 @@
     return [sums[8 * i : 8 * i + 8] for i in range(len(chunks))]
 
 
-def tile_step(scale, q, k, v, g, k_t, decay_col, starts, score, grad, dk, dv, col, dq, rows_sum, t):
+def tile_step(scale, q, k, v, g, k_t, decay_col, starts, score, grad, dk, dv, col, dq, rows_sum, t, saved=None):
     chunks = BAND // TILE
     nt = (((1,), (1,)), ((), ()))
     base = pl.multiple_of(t * TILE, TILE)
@@ -109,7 +109,26 @@
         ds = p * (grad[c] - delta)
         low = ds.astype(BF16)
         col[at, :] += ds[:, :HEAD] + ds[:, HEAD:]
+        if saved is not None:
+            saved[0][t, c] = p.astype(BF16)
+            saved[1][t, c] = low
+            continue
         dv[at, :] += jnp.dot(p.astype(BF16), g_t, preferred_element_type=F32)
+        dk[at, :] += jnp.dot(low, q_t, preferred_element_type=F32)
+        dq_t = dq_t + jnp.dot(k_t[:, at], low, preferred_element_type=F32)
+    if saved is None:
+        dq[mine, :] = (dq_t * scale).T.astype(BF16)
+
+
+def tile_products(scale, q, g, k_t, dk, dv, dq, saved, t):
+    base = pl.multiple_of(t * TILE, TILE)
+    mine = pl.ds(base, TILE)
+    q_t, g_t = q[mine, :], g[mine, :]
+    dq_t = jnp.zeros((HEAD, TILE), F32)
+    for c in range(BAND // TILE):
+        at = pl.ds(base + c * TILE, TILE)
+        low = saved[1][t, c]
+        dv[at, :] += jnp.dot(saved[0][t, c], g_t, preferred_element_type=F32)
         dk[at, :] += jnp.dot(low, q_t, preferred_element_type=F32)
         dq_t = dq_t + jnp.dot(k_t[:, at], low, preferred_element_type=F32)
     dq[mine, :] = (dq_t * scale).T.astype(BF16)
@@ -122,10 +141,10 @@
     qh, kh, vh, gh, parts, part, logits, decay, starts,
     k_t, decay_col, score, grad, dk, dv, col, dq, row_sum, col_sum,
     halo_out, halo_in, low, cols_out, cols_in,
-    gate, inbox, wide, term, first, stage, second, x, x_sem,
+    gate, inbox, wide, term, stage, first, second, x, x_sem, saved_p, saved_s,
     in_send, in_recv, own_in, relay_send, relay_recv, small_send, small_recv,
     out_send, out_recv, own_out, halo_send, halo_recv,
-    g_send, g_recv, y_send, y_recv, z_send, z_recv, w_send, w_recv, v_send, v_recv,
+    g_send, g_recv, z_send, z_recv, y_send, y_recv, w_send, w_recv,
 ):
     scale = HEAD ** (-0.5)
     home, window = RING * rows, RING * rows + HALO
@@ -137,10 +156,10 @@
     peers = [(ring_peer(dp, y, s), tensor) for s in range(1, RING)]
     mates = [(dp, lax.rem(tensor + s, n_tensor)) for s in range(1, n_tensor)]
     line = [(xh * plane + lax.rem(z + s, nz) * RING + y, tensor) for s in range(1, nz)]
-    planes = [
-        (lax.rem(xh + a, nx) * plane + lax.rem(z + b, nz) * RING + y, tensor)
+    sides = [
+        (lax.rem(xh + a, nx) * plane + z * RING + lax.rem(y + b, RING), tensor)
         for a in range(nx)
-        for b in range(nz)
+        for b in range(RING)
     ][1:]
     homes = [
         (ring_peer(dp, y, a), lax.rem(tensor + b, n_tensor)) for a in range(RING) for b in range(n_tensor)
@@ -154,7 +173,7 @@
             gate_weight[...], x[...], (((1,), (1,)), ((), ())), preferred_element_type=F32
         )
 
-    greet(homes + planes, meanwhile)
+    greet(homes + line + sides[RING - 1 :] + [(after, tensor), (before, tensor)], meanwhile)
 
     def columns(shard, h):
         return pl.ds(pl.multiple_of(shard * (2 * HEAD) + h * HEAD, HEAD), HEAD)
@@ -255,12 +274,19 @@
             mine = jnp.where(which == 2 * y + h, decay[:, at], 0.0)
             decay_col[at, :] = jnp.broadcast_to(jnp.sum(mine, axis=0, keepdims=True), (8, 512)).T
 
-    def tiles(h, low_tile, high_tile):
+    def tiles(h, low_tile, high_tile, saved=None):
         def step(t, carry):
             tile_step(
                 scale, qh.at[h], kh.at[h], vh.at[h], gh.at[h], k_t, decay_col, starts, score, grad,
-                dk.at[h], dv.at[h], col.at[h], dq.at[h], row_sum.at[h], t,
+                dk.at[h], dv.at[h], col.at[h], dq.at[h], row_sum.at[h], t, saved,
             )
+            return carry
+
+        lax.fori_loop(low_tile, high_tile, step, 0)
+
+    def products(h, low_tile, high_tile, saved):
+        def step(t, carry):
+            tile_products(scale, qh.at[h], gh.at[h], k_t, dk.at[h], dv.at[h], dq.at[h], saved, t)
             return carry
 
         lax.fori_loop(low_tile, high_tile, step, 0)
@@ -344,12 +370,12 @@
     sum_columns(0)
     prepare(1, range(halo_blocks, blocks))
     arrived(1, (2, 3))
-    tiles(1, half, full)
+    saved = (saved_p, saved_s)
+    tiles(1, half, full, saved)
     for copy in relays_1:
         copy.wait()
     prepare(1, range(halo_blocks))
-    give_far(0)
-    tiles(1, 0, half)
+    tiles(1, 0, half, saved)
 
     sum_columns(1)
     which = lax.broadcasted_iota(jnp.int32, (8, 128), 0)
@@ -363,8 +389,9 @@
         cols_out[:, at] = jnp.where(which == 0, col_sum[0, :, at], col_sum[1, :, at])
     cols_out[:, HALO:] = jnp.where(which == 0, over[0], over[1])
     cols = send(cols_out, cols_in, small, 7, (before, tensor))
+    give_far(0)
+    products(1, 0, half, saved)
     give_halo(1)
-    cast_near(1)
     cols.wait()
 
     pieces, packed = {}, {}
@@ -401,7 +428,9 @@
         send(gate.at[lax.rem(device[0], RING)], inbox.at[slot], (g_send, g_recv), s, device)
         for s, device in enumerate(homes)
     ]
+    products(1, half, full, saved)
     give(dq.at[1], dq_out, 1, 0, (0, RING))
+    cast_near(1)
     give_near(1, (0,))
     inbox[slot] = gate[y]
     for copy in copies:
@@ -410,51 +439,36 @@
         for r in range(8):
             h, c = divmod(r, rows // 128)
             wide[2 * s + h : 2 * s + h + 1, c * 128 : (c + 1) * 128] = inbox[s, r : r + 1, :]
-    width = x.shape[1]
-    term[:, :width] = jnp.dot(wide[...].astype(BF16), x[...], preferred_element_type=F32)
-    for r in range(0, term.shape[0], 8):
-        term[r : r + 8, width:] = jnp.broadcast_to(bias_sum, (8, 128))
-
+    term[...] = jnp.dot(wide[...].astype(BF16), x[...], preferred_element_type=F32)
+    for c in range(nz):
+        stage[c, : term.shape[0], :] = term[:, c * 128 : (c + 1) * 128]
+        stage[c, term.shape[0] :, :] = jnp.broadcast_to(bias_sum, (8, 128))
     copies = [
-        send(
-            term.at[pl.ds(pl.multiple_of(lax.rem(device[0], RING) * 8, 8), 8)],
-            first.at[s], (y_send, y_recv), s, device,
-        )
-        for s, device in enumerate(peers)
+        send(stage.at[lax.rem(device[0], plane) // RING], first.at[s], (z_send, z_recv), s, device)
+        for s, device in enumerate(line)
+    ]
+    piece = stage[z]
+    for s, copy in enumerate(copies):
+        copy.wait()
+        piece = piece + first[s]
+
+    stage[z] = piece
+    copies = [
+        send(stage.at[z], second.at[s], (y_send, y_recv), s, device) for s, device in enumerate(sides)
     ]
     give_near(1, (1,))
-    here = pl.ds(pl.multiple_of(y * 8, 8), 8)
-    part_sum = term[here, :]
-    for s, copy in enumerate(copies):
-        copy.wait()
-        part_sum = part_sum + first[s]
-    for c in range(nz):
-        stage[c, :, :128] = part_sum[:, c * 128 : (c + 1) * 128]
-        stage[c, :, 128:] = part_sum[:, width:]
-
-    copies = [
-        send(stage.at[lax.rem(device[0], plane) // RING], second.at[s], (z_send, z_recv), s, device)
-        for s, device in enumerate(planes)
-    ]
     give_far(1)
-    piece = stage[z]
     for s, copy in enumerate(copies):
         copy.wait()
         piece = piece + second[s]
     eye = which == lax.broadcasted_iota(jnp.int32, (8, 128), 1)
-    bias_out[...] = jnp.sum(jnp.where(eye, piece[:, 128:], 0.0), axis=0, keepdims=True)[:, :8]
+    bias_out[...] = jnp.sum(jnp.where(eye, piece[term.shape[0] :], 0.0), axis=0, keepdims=True)[:, :8]
 
     lanes = pl.ds(pl.multiple_of(z * 128, 128), 128)
-    weight_out[here, lanes] = piece[:, :128]
+    weight_out[:, lanes] = piece[: term.shape[0]]
     copies = [
-        send(weight_out.at[here, lanes], weight_out.at[here, lanes], (w_send, w_recv), s, device)
+        send(weight_out.at[:, lanes], weight_out.at[:, lanes], (w_send, w_recv), s, device)
         for s, device in enumerate(line)
-    ]
-    for copy in copies:
-        copy.wait()
-    copies = [
-        send(weight_out.at[here], weight_out.at[here], (v_send, v_recv), s, device)
-        for s, device in enumerate(peers)
     ]
     for copy in copies:
         copy.wait()
@@ -541,15 +555,16 @@
             pltpu.VMEM((RING, 8, 128), F32),
             pltpu.VMEM((n_tensor * RING, 8, 128), F32),
             pltpu.VMEM((heads, rows), F32),
-            pltpu.VMEM((heads, width + 128), F32),
-            pltpu.VMEM((3, 8, width + 128), F32),
-            pltpu.VMEM((nz, 8, 256), F32),
-            pltpu.VMEM((nx * nz - 1, 8, 256), F32),
+            pltpu.VMEM((heads, width), F32),
+            pltpu.VMEM((nz, heads + 8, 128), F32),
+            pltpu.VMEM((nz - 1, heads + 8, 128), F32),
+            pltpu.VMEM((nx * RING - 1, heads + 8, 128), F32),
             pltpu.VMEM((rows, width), BF16),
             pltpu.SemaphoreType.DMA,
+            *([pltpu.VMEM((home // TILE, chunks, TILE, TILE), BF16)] * 2),
             *dma(24, 24, 8, 4, 4, 8, 8),
             *dma(18, 18, 6, 4, 4),
-            *dma(*[n_tensor * RING - 1] * 2, 3, 3, *[nx * nz - 1] * 2, nz - 1, nz - 1, 3, 3),
+            *dma(*[n_tensor * RING - 1] * 2, *[nz - 1] * 2, *[nx * RING - 1] * 2, *[nz - 1] * 2),
         ],
         compiler_params=pltpu.CompilerParams(
             collective_id=0, has_side_effects=True, vmem_limit_bytes=56 * 2**20

time: 117 us -> 111 us (0.949)
  Pallas kernels: 116 us -> 110 us
    pallas_call x1, Pallas kernels: 113 us -> 107 us  [shards(): pl.pallas_call(functools.partial(main_kernel, rows, n_dp, n_tensor, nz, n...]
where the time goes in v4:
time: 111 us
  Pallas kernels  110 us (99%)
    pallas_call x1, Pallas kernels, shards(): pl.pallas_call(functools.partial(main_kernel, rows, n_dp, n_tensor, nz, n...  107 us
    pallas_call x1, Pallas kernels, finish(): pl.pallas_call(finish_kernel, out_shape=tuple((jax.ShapeDtypeStruct(a.sha...  3.01 us

profile of v4, /device:TPU:24, one launch (start us, length us, event | category | flops | bytes accessed | tf_op | source)
XLA Modules:
  0.0 110.5 jit_solution(12584887751846081498)
XLA Ops:
  0.6 106.9 %main.1 = (bf16[512,1024]{1,0:T(8,128)(2,1)}, bf16[512,1024]{1,0:T(8,128)(2,1)}, bf16[512,1024]{1,0:T(8,128)(2,1)}, f32[32,1024]{1,0:T(8,128)}, f32[1,8]{1,0:T(1,128)}) custom-call(bf16[512,1024]{1,0:T(8,128)(2,1)} %q.1, bf16[512,1024]{1,0:T(8,128)(2,1)} %k.1, bf16[512,1024]{1,0:T(8,128)(2,1)} %v.1, bf16[512,1024]{1,0:T(8,128)(2,1)} %g.1, ...), custom_call_target="tpu_custom_call" | custom-call | tf_op jit(solution)/shard_map/main/pallas_call | solution.py:523
  107.5 3.0 %finish.1 = (bf16[512,1024]{1,0:T(8,128)(2,1)}, bf16[512,1024]{1,0:T(8,128)(2,1)}, bf16[512,1024]{1,0:T(8,128)(2,1)}, f32[32,1024]{1,0:T(8,128)}, f32[1,8]{1,0:T(1,128)}) custom-call(bf16[512,1024]{1,0:T(8,128)(2,1)} %get-tuple-element.15.refs_0_, bf16[512,1024]{1,0:T(8,128)(2,1)} %get-tuple-element.16.refs_1_, bf16[512,1024]{1,0:T(8,128)(2,1)} %get-tuple-element.17.refs_2_, ...), custom_call_target="tpu_custom_call" | custom-call | tf_op jit(solution)/shard_map/finish/pallas_call | solution.py:496

commit v5 on v4

--- a/solution.py
+++ b/solution.py
@@ -203,11 +203,11 @@
             for s in range(1, RING):
                 arrive[h, a, s].wait()
 
-    def relay(h):
+    def relay(h, arrays):
         tail = pl.ds(home, HALO)
         return [
             send(ref.at[h, tail], ref.at[h, pl.ds(0, HALO)], (relay_send, relay_recv), h * 2 + a, (after, tensor))
-            for a, ref in enumerate((kh, vh))
+            for a, ref in [(a, (kh, vh)[a]) for a in arrays]
         ]
 
 
@@ -254,7 +254,7 @@
         dv[h] = jnp.zeros((window, HEAD), F32)
         col[h] = jnp.zeros((window, HEAD), F32)
     arrived(0, (0, 1))
-    relays = relay(0)
+    relays = relay(0, (0, 1))
     ahead.wait()
     pieces = []
     for s in range(6):
@@ -343,12 +343,13 @@
             ).astype(BF16)
             give(low.at[h, a], out, h, a + 1, far)
 
-    def sum_columns(h):
-        col_sum[h] = lax.dot_general(
-            jnp.ones((8, HEAD), F32), col[h], (((1,), (1,)), ((), ())),
+    def sum_columns(h, at):
+        col_sum[h, :, at] = lax.dot_general(
+            jnp.ones((8, HEAD), F32), col[h, at], (((1,), (1,)), ((), ())),
             precision=lax.Precision.HIGHEST, preferred_element_type=F32,
         )
 
+    behind, within = slice(0, HALO), slice(HALO, window)
     blocks = window // 512
     halo_blocks = HALO // 512
     half = HALO // TILE
@@ -356,66 +357,73 @@
     prepare(0, range(halo_blocks, blocks))
     arrived(0, (2, 3))
     tiles(0, half, full)
+    arrived(1, (0,))
+    relays_1 = relay(1, (0,))
     for copy in relays:
         copy.wait()
     prepare(0, range(halo_blocks))
     tiles(0, 0, half // 2)
-    arrived(1, (0, 1))
-    relays_1 = relay(1)
+    arrived(1, (1,))
+    relays_1 += relay(1, (1,))
     tiles(0, half // 2, half)
     give_halo(0)
     cast_near(0)
     give(dq.at[0], dq_out, 0, 0, (0, RING))
     give_near(0)
-    sum_columns(0)
+    sum_columns(0, behind)
+    sum_columns(0, within)
     prepare(1, range(halo_blocks, blocks))
     arrived(1, (2, 3))
     saved = (saved_p, saved_s)
-    tiles(1, half, full, saved)
     for copy in relays_1:
         copy.wait()
     prepare(1, range(halo_blocks))
     tiles(1, 0, half, saved)
 
-    sum_columns(1)
+    sum_columns(1, behind)
     which = lax.broadcasted_iota(jnp.int32, (8, 128), 0)
-    crossed = starts[...] < HALO
-    over = []
-    for h in range(2):
-        here = jnp.where(crossed, row_sum[h] - col_sum[h, :, HALO:], 0.0)
-        over.append(jnp.broadcast_to(jnp.sum(here, axis=1, keepdims=True), (8, 128)))
     for c in range(HALO // 128):
         at = slice(c * 128, (c + 1) * 128)
         cols_out[:, at] = jnp.where(which == 0, col_sum[0, :, at], col_sum[1, :, at])
-    cols_out[:, HALO:] = jnp.where(which == 0, over[0], over[1])
     cols = send(cols_out, cols_in, small, 7, (before, tensor))
-    give_far(0)
-    products(1, 0, half, saved)
-    give_halo(1)
-    cols.wait()
-
-    pieces, packed = {}, {}
-    bias_sum = jnp.zeros((8, 1), F32)
+    tiles(1, half, full, saved)
+    sum_columns(1, within)
+
+    pieces, falls = {}, {}
     for h in range(2):
         for c in range(home // 128):
             at = slice(c * 128, (c + 1) * 128)
-            piece = row_sum[h, :, at] - col_sum[h, :, HALO + c * 128 : HALO + (c + 1) * 128]
-            if c * 128 >= split:
-                off = c * 128 - split
-                piece = piece - cols_in[h : h + 1, off : off + 128]
-            pieces[h, c] = piece
-    sums = dict(zip(pieces, running(list(pieces.values()), True)))
-    for h in range(2):
-        carry = cols_in[h : h + 1, HALO : HALO + 1]
-        mine_of = jnp.zeros((8, 1), F32)
-        for c in reversed(range(home // 128)):
+            pieces[h, c] = row_sum[h, :, at] - col_sum[h, :, HALO + c * 128 : HALO + (c + 1) * 128]
             shard, off = divmod(c * 128, rows)
-            keep = sums[h, c] + carry
-            carry = carry + sums[h, c][:, 0:1]
             raw = logits[2 + shard, :, off : off + 128]
             raw = jnp.sum(jnp.where(which == 2 * y + h, raw, 0.0), axis=0, keepdims=True)
             down = jnp.exp(-jnp.abs(raw))
-            gate_grad = keep * (jnp.where(raw >= 0, down, 1.0) / (1.0 + down))
+            falls[h, c] = jnp.where(raw >= 0, down, 1.0) / (1.0 + down)
+    sums = dict(zip(pieces, running(list(pieces.values()), True)))
+    keeps = {}
+    for h in range(2):
+        carry = jnp.zeros((8, 1), F32)
+        for c in reversed(range(home // 128)):
+            keeps[h, c] = sums[h, c] + carry
+            carry = carry + sums[h, c][:, 0:1]
+    cols.wait()
+    ahead_of = running([cols_in[:, c * 128 : (c + 1) * 128] for c in range(HALO // 128)], False)
+    bias_sum = jnp.zeros((8, 1), F32)
+    packed = {}
+    before_it = jnp.zeros((8, 1), F32)
+    share = {}
+    for c in range(home // 128):
+        if c * 128 < split:
+            share[c] = jnp.zeros((8, 128), F32)
+        else:
+            i = (c * 128 - split) // 128
+            share[c] = ahead_of[i] - cols_in[:, i * 128 : (i + 1) * 128] + before_it
+            before_it = before_it + ahead_of[i][:, 127:128]
+    for h in range(2):
+        mine_of = jnp.zeros((8, 1), F32)
+        for c in range(home // 128):
+            shard, off = divmod(c * 128, rows)
+            gate_grad = (keeps[h, c] + share[c][h : h + 1, :]) * falls[h, c]
             mine_of = mine_of + jnp.sum(gate_grad, axis=1, keepdims=True)
             row = h * (rows // 128) + off // 128
             packed[shard] = jnp.where(which == row, gate_grad, packed.get(shard, 0.0))
@@ -428,6 +436,9 @@
         send(gate.at[lax.rem(device[0], RING)], inbox.at[slot], (g_send, g_recv), s, device)
         for s, device in enumerate(homes)
     ]
+    give_far(0)
+    products(1, 0, half, saved)
+    give_halo(1)
     products(1, half, full, saved)
     give(dq.at[1], dq_out, 1, 0, (0, RING))
     cast_near(1)
@@ -443,35 +454,49 @@
     for c in range(nz):
         stage[c, : term.shape[0], :] = term[:, c * 128 : (c + 1) * 128]
         stage[c, term.shape[0] :, :] = jnp.broadcast_to(bias_sum, (8, 128))
+    heads = term.shape[0]
+    parts_of = [pl.ds(0, heads // 2), pl.ds(heads // 2, heads // 2 + 8)]
+    lanes = pl.ds(pl.multiple_of(z * 128, 128), 128)
     copies = [
-        send(stage.at[lax.rem(device[0], plane) // RING], first.at[s], (z_send, z_recv), s, device)
-        for s, device in enumerate(line)
+        [
+            send(
+                stage.at[lax.rem(device[0], plane) // RING, part_of], first.at[s, part_of],
+                (z_send, z_recv), i * len(line) + s, device,
+            )
+            for s, device in enumerate(line)
+        ]
+        for i, part_of in enumerate(parts_of)
     ]
-    piece = stage[z]
-    for s, copy in enumerate(copies):
-        copy.wait()
-        piece = piece + first[s]
-
-    stage[z] = piece
-    copies = [
-        send(stage.at[z], second.at[s], (y_send, y_recv), s, device) for s, device in enumerate(sides)
-    ]
+
+    for i, part_of in enumerate(parts_of):
+        piece = stage[z, part_of]
+        for s, copy in enumerate(copies[i]):
+            copy.wait()
+            piece = piece + first[s, part_of]
+        stage[z, part_of] = piece
+        copies[i] = [
+            send(stage.at[z, part_of], second.at[s, part_of], (y_send, y_recv), i * len(sides) + s, device)
+            for s, device in enumerate(sides)
+        ]
     give_near(1, (1,))
     give_far(1)
-    for s, copy in enumerate(copies):
-        copy.wait()
-        piece = piece + second[s]
+
+    for i, part_of in enumerate(parts_of):
+        piece = stage[z, part_of]
+        for s, copy in enumerate(copies[i]):
+            copy.wait()
+            piece = piece + second[s, part_of]
+        at = pl.ds(i * (heads // 2), heads // 2)
+        weight_out[at, lanes] = piece[: heads // 2]
+        copies[i] = [
+            send(weight_out.at[at, lanes], weight_out.at[at, lanes], (w_send, w_recv), i * len(line) + s, device)
+            for s, device in enumerate(line)
+        ]
     eye = which == lax.broadcasted_iota(jnp.int32, (8, 128), 1)
-    bias_out[...] = jnp.sum(jnp.where(eye, piece[term.shape[0] :], 0.0), axis=0, keepdims=True)[:, :8]
-
-    lanes = pl.ds(pl.multiple_of(z * 128, 128), 128)
-    weight_out[:, lanes] = piece[: term.shape[0]]
-    copies = [
-        send(weight_out.at[:, lanes], weight_out.at[:, lanes], (w_send, w_recv), s, device)
-        for s, device in enumerate(line)
-    ]
-    for copy in copies:
-        copy.wait()
+    bias_out[...] = jnp.sum(jnp.where(eye, piece[heads // 2 :], 0.0), axis=0, keepdims=True)[:, :8]
+    for part in copies:
+        for copy in part:
+            copy.wait()
     for copy in leave:
         copy.wait()
 
@@ -480,15 +505,23 @@
     count = len(refs) // 3
     ins, outs, held = refs[:count], refs[count : 2 * count], refs[2 * count : 3 * count]
     load, store = refs[3 * count :]
-    loads = [pltpu.make_async_copy(ins[i], held[i], load.at[i]) for i in range(count)]
-    stores = [pltpu.make_async_copy(held[i], outs[i], store.at[i]) for i in range(count)]
-    for copy in loads:
+    pairs = []
+    for i in range(count):
+        rows = ins[i].shape[0]
+        step = max(rows // 4, min(rows, 128))
+        for r in range(0, rows, step):
+            at, n = pl.ds(r, step), len(pairs)
+            pairs.append((
+                pltpu.make_async_copy(ins[i].at[at], held[i].at[at], load.at[n]),
+                pltpu.make_async_copy(held[i].at[at], outs[i].at[at], store.at[n]),
+            ))
+    for copy, _ in pairs:
         copy.start()
-    for i in range(count):
-        loads[i].wait()
-        stores[i].start()
-    for copy in stores:
+    for copy, then in pairs:
         copy.wait()
+        then.start()
+    for _, then in pairs:
+        then.wait()
 
 
 def finish(*arrays):
@@ -499,7 +532,7 @@
         in_specs=[hbm] * len(arrays),
         out_specs=(hbm,) * len(arrays),
         scratch_shapes=[pltpu.VMEM(a.shape, a.dtype) for a in arrays]
-        + [pltpu.SemaphoreType.DMA((len(arrays),))] * 2,
+        + [pltpu.SemaphoreType.DMA((4 * len(arrays),))] * 2,
         compiler_params=pltpu.CompilerParams(vmem_limit_bytes=56 * 2**20),
         name="finish",
     )(*arrays)
@@ -550,8 +583,8 @@
             pltpu.VMEM((2, 2, HALO, HEAD), BF16),
             pltpu.VMEM((2, 2, HALO, HEAD), BF16),
             pltpu.VMEM((2, 2, home, HEAD), BF16),
-            pltpu.VMEM((8, HALO + 128), F32),
-            pltpu.VMEM((8, HALO + 128), F32),
+            pltpu.VMEM((8, HALO), F32),
+            pltpu.VMEM((8, HALO), F32),
             pltpu.VMEM((RING, 8, 128), F32),
             pltpu.VMEM((n_tensor * RING, 8, 128), F32),
             pltpu.VMEM((heads, rows), F32),
@@ -564,7 +597,7 @@
             *([pltpu.VMEM((home // TILE, chunks, TILE, TILE), BF16)] * 2),
             *dma(24, 24, 8, 4, 4, 8, 8),
             *dma(18, 18, 6, 4, 4),
-            *dma(*[n_tensor * RING - 1] * 2, *[nz - 1] * 2, *[nx * RING - 1] * 2, *[nz - 1] * 2),
+            *dma(*[n_tensor * RING - 1] * 2, *[2 * nz - 2] * 2, *[2 * nx * RING - 2] * 2, *[2 * nz - 2] * 2),
         ],
         compiler_params=pltpu.CompilerParams(
             collective_id=0, has_side_effects=True, vmem_limit_bytes=56 * 2**20

time: 111 us -> 107 us (0.964)
  Pallas kernels: 110 us -> 107 us
    pallas_call x1, Pallas kernels: 107 us -> 104 us  [shards(): pl.pallas_call(functools.partial(main_kernel, rows, n_dp, n_tensor, nz, n...]
where the time goes in v5:
time: 107 us
  Pallas kernels  107 us (100%)
    pallas_call x1, Pallas kernels, shards(): pl.pallas_call(functools.partial(main_kernel, rows, n_dp, n_tensor, nz, n...  104 us
    pallas_call x1, Pallas kernels, finish(): pl.pallas_call(finish_kernel, out_shape=tuple((jax.ShapeDtypeStruct(a.sha...  2.99 us

profile of v5, /device:TPU:24, one launch (start us, length us, event | category | flops | bytes accessed | tf_op | source)
XLA Modules:
  0.0 107.2 jit_solution(709761251599458141)
XLA Ops:
  0.6 103.6 %main.1 = (bf16[512,1024]{1,0:T(8,128)(2,1)}, bf16[512,1024]{1,0:T(8,128)(2,1)}, bf16[512,1024]{1,0:T(8,128)(2,1)}, f32[32,1024]{1,0:T(8,128)}, f32[1,8]{1,0:T(1,128)}) custom-call(bf16[512,1024]{1,0:T(8,128)(2,1)} %q.1, bf16[512,1024]{1,0:T(8,128)(2,1)} %k.1, bf16[512,1024]{1,0:T(8,128)(2,1)} %v.1, bf16[512,1024]{1,0:T(8,128)(2,1)} %g.1, ...), custom_call_target="tpu_custom_call" | custom-call | tf_op jit(solution)/shard_map/main/pallas_call | solution.py:556
  104.2 3.0 %finish.1 = (bf16[512,1024]{1,0:T(8,128)(2,1)}, bf16[512,1024]{1,0:T(8,128)(2,1)}, bf16[512,1024]{1,0:T(8,128)(2,1)}, f32[32,1024]{1,0:T(8,128)}, f32[1,8]{1,0:T(1,128)}) custom-call(bf16[512,1024]{1,0:T(8,128)(2,1)} %get-tuple-element.15.refs_0_, bf16[512,1024]{1,0:T(8,128)(2,1)} %get-tuple-element.16.refs_1_, bf16[512,1024]{1,0:T(8,128)(2,1)} %get-tuple-element.17.refs_2_, ...), custom_call_target="tpu_custom_call" | custom-call | tf_op jit(solution)/shard_map/finish/pallas_call | solution.py:529

commit v6 on v5

--- a/solution.py
+++ b/solution.py
@@ -216,7 +216,7 @@
         send(part.at[pl.ds(pl.multiple_of(mate[1] * 8, 8), 8)], parts.at[s], small, s, mate)
         for s, mate in enumerate(mates)
     ]
-    fetch(0, (0,))
+    fetch(0, (0, 1))
     eye = lax.broadcasted_iota(jnp.int32, (8, 8), 0) == lax.broadcasted_iota(jnp.int32, (8, 8), 1)
     bias = jnp.sum(
         jnp.where(eye, jnp.broadcast_to(gate_bias[...], (8, 8)), 0.0), axis=1, keepdims=True
@@ -230,7 +230,7 @@
     spread = [
         send(logits.at[2 + y], logits.at[2 + y], small, 3 + s, peer) for s, peer in enumerate(peers)
     ]
-    fetch(0, (1, 2, 3))
+    fetch(0, (2, 3))
     fetch(1, range(4))
     docs = lengths.shape[1]
     at_0 = lax.broadcasted_iota(jnp.int32, (docs, docs), 0)

time: 107 us -> 107 us (level)
  no operation moved by 1% of the time
where the time goes in v6:
time: 107 us
  Pallas kernels  107 us (100%)
    pallas_call x1, Pallas kernels, shards(): pl.pallas_call(functools.partial(main_kernel, rows, n_dp, n_tensor, nz, n...  104 us
    pallas_call x1, Pallas kernels, finish(): pl.pallas_call(finish_kernel, out_shape=tuple((jax.ShapeDtypeStruct(a.sha...  2.99 us

profile of v6, /device:TPU:24, one launch (start us, length us, event | category | flops | bytes accessed | tf_op | source)
XLA Modules:
  0.0 107.2 jit_solution(14093879902525760681)
XLA Ops:
  0.6 103.6 %main.1 = (bf16[512,1024]{1,0:T(8,128)(2,1)}, bf16[512,1024]{1,0:T(8,128)(2,1)}, bf16[512,1024]{1,0:T(8,128)(2,1)}, f32[32,1024]{1,0:T(8,128)}, f32[1,8]{1,0:T(1,128)}) custom-call(bf16[512,1024]{1,0:T(8,128)(2,1)} %q.1, bf16[512,1024]{1,0:T(8,128)(2,1)} %k.1, bf16[512,1024]{1,0:T(8,128)(2,1)} %v.1, bf16[512,1024]{1,0:T(8,128)(2,1)} %g.1, ...), custom_call_target="tpu_custom_call" | custom-call | tf_op jit(solution)/shard_map/main/pallas_call | solution.py:556
  104.2 3.0 %finish.1 = (bf16[512,1024]{1,0:T(8,128)(2,1)}, bf16[512,1024]{1,0:T(8,128)(2,1)}, bf16[512,1024]{1,0:T(8,128)(2,1)}, f32[32,1024]{1,0:T(8,128)}, f32[1,8]{1,0:T(1,128)}) custom-call(bf16[512,1024]{1,0:T(8,128)(2,1)} %get-tuple-element.15.refs_0_, bf16[512,1024]{1,0:T(8,128)(2,1)} %get-tuple-element.16.refs_1_, bf16[512,1024]{1,0:T(8,128)(2,1)} %get-tuple-element.17.refs_2_, ...), custom_call_target="tpu_custom_call" | custom-call | tf_op jit(solution)/shard_map/finish/pallas_call | solution.py:529
